TPU v7x, 32 devices: a whole 2x2x4 slice. The times are simulated.
32 devices in a mesh: parts: 2 (over y), expert: 4 (over x, core), tensor: 4 (over z).
Axes of the slice: x: 2, y: 2, z: 4, core: 2. Of those that a mesh axis runs over, the one named last changes fastest.
Arguments:
- tokens: bfloat16 [32, 3072], P(('parts', 'expert', 'tensor')), parts along dimension 0, may hold values from -6 to 6
- cotangent: bfloat16 [32, 3072], P(('parts', 'expert', 'tensor')), parts along dimension 0, may hold values from -6 to 6
- routes: int32 [32, 2], P(('parts', 'expert')), parts along dimension 0, may hold values from 0 to 3, all different within a row; in each aligned block of 4 rows (0 to 3, 4 to 7, ...) at most 2 rows name the same one
- router: bfloat16 [3072, 4], replicated, may hold values from -0.109375 to 0.109375
- w_gate: bfloat16 [4, 3072, 16384], P('expert', None, 'tensor'), may hold values from -0.109375 to 0.109375
- w_up: bfloat16 [4, 3072, 16384], P('expert', None, 'tensor'), may hold values from -0.109375 to 0.109375
- w_down: bfloat16 [4, 16384, 3072], P('expert', 'tensor'), may hold values from -0.046875 to 0.046875
- adapter_down: bfloat16 [4, 3072, 32], P('expert', 'tensor'), may hold values from -0.109375 to 0.109375
- adapter_up: bfloat16 [4, 2, 16, 16384], P('expert', None, None, 'tensor'), may hold values from -1.5 to 1.5
Outputs:
- grad_tokens: bfloat16 [32, 3072], P(('parts', 'expert', 'tensor')), parts along dimension 0
- grad_down: float32 [8, 3072, 32], P(('parts', 'expert'), 'tensor'), parts along dimension 0
- grad_up: float32 [8, 2, 16, 16384], P(('parts', 'expert'), None, None, 'tensor'), parts along dimension 0
There are 2 independent parts, one for each index of `parts`. A program takes and returns all parts, laid end to end along the dimension named above; an argument that names none is the same for every part. Nothing has to cross between parts.
Inputs may be any that keep to these rules, and one draw needn't show every extreme that they name: The two routes of a token differ. In each aligned block of 4 rows no expert is named by more than 2 routes, and some block reaches 2.
All inputs are finite; a program needn't handle non-finite values.
Results may differ from a plain program's by a relative error of at most 0.006.
Values may be sent and summed in bfloat16 or wider, within the bound.
No kernel may reach another device: no remote copies, remote signals or barrier semaphores. Data moves between devices by JAX's collectives and lax.ppermute only.
A program may use at most 192 MiB of HBM per device.

v0:
```python
import jax
import jax.numpy as jnp
from jax import lax
from jax.sharding import PartitionSpec as P

adapter_scale = 0.5


def slot_index(group_routes, experts, capacity):
    flat_routes = group_routes.reshape(-1)
    one_hot = (flat_routes[:, None] == jnp.arange(experts, dtype=jnp.int32)[None, :]).astype(
        jnp.int32
    )
    earlier = jnp.cumsum(one_hot, axis=0) - one_hot
    position = jnp.sum(earlier * one_hot, axis=1)
    return (flat_routes * capacity + position).reshape(group_routes.shape)


def per_device(tokens, cotangent, routes, router, w_gate, w_up, w_down, adapter_down, adapter_up):
    expert_size = lax.axis_size("expert")
    tensor_index = lax.axis_index("tensor")
    experts = router.shape[1]
    model_width = tokens.shape[1]
    tok_count = tokens.shape[0]
    size_group = routes.shape[0]
    capacity = 2 * size_group // experts * 5 // 4
    rank_size = adapter_up.shape[2]
    col_width = adapter_down.shape[1]
    first_row = tensor_index * tok_count
    first_col = tensor_index * col_width
    group_x, group_cot = (
        lax.all_gather(tokens, "tensor", axis=0, tiled=True),
        lax.all_gather(cotangent, "tensor", axis=0, tiled=True),
    )
    logits = jnp.dot(group_x, router, preferred_element_type=jnp.float32)
    picked = jnp.take_along_axis(logits, routes, axis=1)
    chance = jax.nn.sigmoid(picked[:, 0] - picked[:, 1])
    gate_vals = jnp.stack([chance, 1.0 - chance], axis=1).astype(jnp.bfloat16)
    positions = slot_index(routes, experts, capacity)
    matches = (
        positions.reshape(1, size_group, 2)
        == jnp.arange(experts * capacity, dtype=jnp.int32)[:, None, None]
    )
    dispatch_mat = jnp.sum(matches.astype(jnp.float32), axis=2).astype(jnp.bfloat16)
    slot_x = jnp.dot(dispatch_mat, group_x, preferred_element_type=jnp.float32).astype(jnp.bfloat16)
    slot_cot = jnp.dot(dispatch_mat, group_cot, preferred_element_type=jnp.float32).astype(
        jnp.bfloat16
    )
    slot_gate = jnp.sum(
        matches.astype(jnp.float32) * gate_vals.astype(jnp.float32)[None, :, :], axis=(1, 2)
    ).astype(jnp.bfloat16)
    recv_x, recv_cot, recv_gate = (
        lax.all_to_all(
            slot_x.reshape(experts, capacity, model_width),
            "expert",
            split_axis=0,
            concat_axis=0,
            tiled=True,
        ),
        lax.all_to_all(
            slot_cot.reshape(experts, capacity, model_width),
            "expert",
            split_axis=0,
            concat_axis=0,
            tiled=True,
        ),
        lax.all_to_all(
            slot_gate.reshape(experts, capacity), "expert", split_axis=0, concat_axis=0, tiled=True
        ),
    )
    expert_rows = recv_x.reshape(expert_size * capacity, model_width)
    expert_cot = recv_cot.reshape(expert_size * capacity, model_width)
    expert_gate = recv_gate.reshape(expert_size * capacity)
    gate_mat = w_gate[0]
    up_mat = w_up[0]
    down_mat = w_down[0]
    adapt_in = adapter_down[0]
    adapt_out = adapter_up[0]
    expert_cols = lax.dynamic_slice_in_dim(expert_rows, first_col, col_width, 1)
    whole_in = lax.all_gather(adapt_in, "tensor", axis=0, tiled=True)
    latent = jnp.dot(expert_rows, whole_in, preferred_element_type=jnp.float32).astype(jnp.bfloat16)
    latent_gate = latent[:, :rank_size]
    latent_up = latent[:, rank_size:]
    gate_pre = jnp.dot(
        expert_rows, gate_mat, preferred_element_type=jnp.float32
    ) + adapter_scale * jnp.dot(latent_gate, adapt_out[0], preferred_element_type=jnp.float32)
    up_pre = jnp.dot(
        expert_rows, up_mat, preferred_element_type=jnp.float32
    ) + adapter_scale * jnp.dot(latent_up, adapt_out[1], preferred_element_type=jnp.float32)
    sigmoid_gate = jax.nn.sigmoid(gate_pre)
    activated = gate_pre * sigmoid_gate
    hidden = activated * up_pre
    contract = (((1,), (1,)), ((), ()))
    returned = lax.dot_general(expert_cot, down_mat, contract, preferred_element_type=jnp.float32)
    gate_share = jnp.sum(returned * hidden, axis=1)
    d_hidden = expert_gate.astype(jnp.float32)[:, None] * returned
    d_gate_pre = (
        d_hidden * up_pre * sigmoid_gate * (1.0 + gate_pre * (1.0 - sigmoid_gate))
    ).astype(jnp.bfloat16)
    d_up_pre = (d_hidden * activated).astype(jnp.bfloat16)
    latent_share_grad = adapter_scale * jnp.concatenate(
        [
            lax.dot_general(d_gate_pre, adapt_out[0], contract, preferred_element_type=jnp.float32),
            lax.dot_general(d_up_pre, adapt_out[1], contract, preferred_element_type=jnp.float32),
        ],
        axis=1,
    )
    latent_total, gate_total = lax.psum((latent_share_grad, gate_share), "tensor")
    d_latent = latent_total.astype(jnp.bfloat16)
    rows_contract = (((0,), (0,)), ((), ()))
    grad_down = lax.dot_general(
        expert_cols, d_latent, rows_contract, preferred_element_type=jnp.float32
    )
    grad_up = jnp.stack(
        [
            adapter_scale
            * lax.dot_general(
                latent_gate, d_gate_pre, rows_contract, preferred_element_type=jnp.float32
            ),
            adapter_scale
            * lax.dot_general(
                latent_up, d_up_pre, rows_contract, preferred_element_type=jnp.float32
            ),
        ],
        axis=0,
    )
    d_rows = lax.dot_general(d_gate_pre, gate_mat, contract, preferred_element_type=jnp.float32)
    d_rows = d_rows + lax.dot_general(
        d_up_pre, up_mat, contract, preferred_element_type=jnp.float32
    )
    adapter_cols = lax.dot_general(d_latent, adapt_in, contract, preferred_element_type=jnp.float32)
    own_block = lax.dynamic_slice_in_dim(d_rows, first_col, col_width, 1) + adapter_cols
    d_rows = lax.dynamic_update_slice_in_dim(d_rows, own_block, first_col, 1)
    flat_slots = positions.reshape(-1)
    shares = lax.psum_scatter(
        d_rows.reshape(expert_size, capacity, model_width),
        "tensor",
        scatter_dimension=2,
        tiled=True,
    )
    back_cols, back_gate = (
        lax.all_to_all(shares, "expert", split_axis=0, concat_axis=0, tiled=True),
        lax.all_to_all(
            gate_total.reshape(expert_size, capacity),
            "expert",
            split_axis=0,
            concat_axis=0,
            tiled=True,
        ),
    )
    route_cols = jnp.take(back_cols.reshape(experts * capacity, col_width), flat_slots, axis=0)
    token_cols = route_cols.reshape(size_group, 2, col_width).sum(axis=1)
    token_grad = lax.all_to_all(token_cols, "tensor", split_axis=0, concat_axis=1, tiled=True)
    route_grads = jnp.take(back_gate.reshape(experts * capacity), flat_slots, axis=0).reshape(
        size_group, 2
    )
    own_grads = lax.dynamic_slice_in_dim(route_grads, first_row, tok_count, 0)
    own_chance = lax.dynamic_slice_in_dim(chance, first_row, tok_count, 0)
    own_routes = lax.dynamic_slice_in_dim(routes, first_row, tok_count, 0)
    d_gap = (own_grads[:, 0] - own_grads[:, 1]) * own_chance * (1.0 - own_chance)
    expert_ids = jnp.arange(experts, dtype=jnp.int32)[None, :]
    d_logits = (
        (own_routes[:, 0:1] == expert_ids).astype(jnp.float32)
        - (own_routes[:, 1:2] == expert_ids).astype(jnp.float32)
    ) * d_gap[:, None]
    grad_tokens = token_grad + jnp.dot(
        d_logits, router.astype(jnp.float32).T, precision=lax.Precision.HIGHEST
    )
    return (grad_tokens.astype(jnp.bfloat16), grad_down[None], grad_up[None])


def solution(mesh):
    return jax.shard_map(
        per_device,
        mesh=mesh,
        in_specs=(
            P(("parts", "expert", "tensor"), None),
            P(("parts", "expert", "tensor"), None),
            P(("parts", "expert"), None),
            P(),
            P("expert", None, "tensor"),
            P("expert", None, "tensor"),
            P("expert", "tensor", None),
            P("expert", "tensor", None),
            P("expert", None, None, "tensor"),
        ),
        out_specs=(
            P(("parts", "expert", "tensor"), None),
            P(("parts", "expert"), "tensor", None),
            P(("parts", "expert"), None, None, "tensor"),
        ),
        check_vma=False,
    )
```

profile of v0, /device:TPU:0, one launch (start us, length us, event | category | flops | bytes accessed | tf_op | source)
XLA Modules:
  0.0 213.6 jit_solution(3161792285706951803)
XLA Ops:
  8.6 14.9 %all-gather.1 = bf16[4,1,3072]{2,1,0:T(2,128)(2,1)S(1)} all-gather(bf16[1,1,3072]{2,1,0:T(2,128)(2,1)} %bitcast.92), channel_id=1, replica_groups=mesh['parts'=2,'expert'=4,'tensor'=4] {'tensor'}, dimensions={0}, use_global_device_ids=true | all-gather | bytes 30720 | tf_op jit(solution)/shard_map/all_gather | solution.py:32
  25.6 3.2 %all-to-all-start = ((bf16[4,1,2]{2,1,0:T(2,128)(2,1)}), bf16[4,1,2]{2,1,0:T(2,128)(2,1)S(1)}, u32[]{:S(2)}, u32[]{:S(2)}) async-start(bf16[4,1,2]{2,1,0:T(2,128)(2,1)} %convert_element_type.102), calls=%async_computation | async-start | bytes 4096 | tf_op jit(solution)/shard_map/all_to_all | solution.py:67
  29.7 13.9 %all-gather = bf16[1,3072,32]{1,2,0:T(8,128)(2,1)S(1)} all-gather(bf16[1,768,32]{1,2,0:T(8,128)(2,1)} %param.16), channel_id=2, replica_groups=mesh['parts'=2,'expert'=4,'tensor'=4] {'tensor'}, dimensions={1}, use_global_device_ids=true | all-gather | bytes 245760 | tf_op jit(solution)/shard_map/all_gather | solution.py:80
  43.7 13.3 %all-gather.2 = bf16[4,1,3072]{2,1,0:T(2,128)(2,1)S(1)} all-gather(bf16[1,1,3072]{2,1,0:T(2,128)(2,1)} %bitcast.93), channel_id=1, replica_groups=mesh['parts'=2,'expert'=4,'tensor'=4] {'tensor'}, dimensions={0}, use_global_device_ids=true | all-gather | bytes 30720 | tf_op jit(solution)/shard_map/all_gather | solution.py:33
  59.9 3.3 %all-to-all-start.2 = ((bf16[4,2,3072]{2,1,0:T(2,128)(2,1)}), bf16[4,2,3072]{2,1,0:T(2,128)(2,1)S(1)}, u32[]{:S(2)}, u32[]{:S(2)}) async-start(bf16[4,2,3072]{2,1,0:T(2,128)(2,1)} %reshape.177), calls=%async_computation.2 | async-start | bytes 98304 | tf_op jit(solution)/shard_map/all_to_all | solution.py:53
  63.8 3.4 %all-to-all-done.2 = bf16[4,2,3072]{2,1,0:T(2,128)(2,1)S(1)} async-done(((bf16[4,2,3072]{2,1,0:T(2,128)(2,1)}), bf16[4,2,3072]{2,1,0:T(2,128)(2,1)S(1)}, u32[]{:S(2)}, u32[]{:S(2)}) %all-to-all-start.2) | async-done | bytes 49184 | tf_op jit(solution)/shard_map/all_to_all | solution.py:53
  67.2 3.9 %all-to-all-start.1 = ((bf16[4,2,3072]{2,1,0:T(2,128)(2,1)}), bf16[4,2,3072]{2,1,0:T(2,128)(2,1)}, u32[]{:S(2)}, u32[]{:S(2)}) async-start(bf16[4,2,3072]{2,1,0:T(2,128)(2,1)} %reshape.175), calls=%async_computation.1 | async-start | bytes 98304 | tf_op jit(solution)/shard_map/all_to_all | solution.py:60
  71.3 10.1 %fusion.2 = f32[8,4096]{1,0:T(8,128)S(1)} fusion(bf16[8,3072]{1,0:T(8,128)(2,1)S(1)} %reshape.178, bf16[1,3072,4096]{2,1,0:T(8,128)(2,1)} %param.13), kind=kOutput, calls=%fused_computation.5 | convolution fusion | flops 201326592 | bytes 25346048 | tf_op jit(solution)/shard_map/dot_general | solution.py:84
  81.3 5.1 %copy-done.1 = bf16[1,3072,4096]{2,1,0:T(8,128)(2,1)S(1)} copy-done((bf16[1,3072,4096]{2,1,0:T(8,128)(2,1)S(1)}, bf16[1,3072,4096]{2,1,0:T(8,128)(2,1)}, u32[]{:S(2)}) %copy-start.1) | copy-done | bytes 25165848
  86.4 3.3 %fusion.6 = f32[8,4096]{1,0:T(8,128)S(1)} fusion(bf16[8,3072]{1,0:T(8,128)(2,1)S(1)} %reshape.178, bf16[1,3072,4096]{2,1,0:T(8,128)(2,1)S(1)} %copy-done.1), kind=kOutput, calls=%fused_computation.9 | convolution fusion | flops 201326592 | bytes 25346048 | tf_op jit(solution)/shard_map/dot_general | solution.py:87
  91.0 11.7 %multiply_reduce_fusion = (f32[8]{0:T(128)S(1)}, bf16[8,4096]{1,0:T(8,128)(2,1)S(1)}, bf16[8,4096]{1,0:T(8,128)(2,1)S(1)}) fusion(f32[8,4096]{1,0:T(8,128)S(1)} %fusion.13, f32[8,4096]{1,0:T(8,128)S(1)} %fusion.12, f32[8]{0:T(128)} %reshape.182, bf16[8,3072]{1,0:T(8,128)(2,1)S(1)} %reshape.176, bf16[1,4096,3072]{2,1,0:T(8,128)(2,1)} %param.15), kind=kOutput, calls=%fused_computation.36 | convolution fusion | flops 201883648 | bytes 25608256 | tf_op jit(solution)/shard_map/dot_general | solution.py:94
  102.9 11.5 %fusion = f32[8,3072]{1,0:T(8,128)S(1)} fusion(bf16[8,4096]{1,0:T(8,128)(2,1)S(1)} %get-tuple-element.12, bf16[1,3072,4096]{2,1,0:T(8,128)(2,1)} %param.13), kind=kOutput, calls=%fused_computation.3 | convolution fusion | flops 201326592 | bytes 25329664 | tf_op jit(solution)/shard_map/dot_general | solution.py:127
  115.2 11.6 %fusion.14 = f32[8,3072]{1,0:T(8,128)S(1)} fusion(f32[8,3072]{1,0:T(8,128)S(1)} %fusion, bf16[8,4096]{1,0:T(8,128)(2,1)S(1)} %get-tuple-element.13, bf16[1,3072,4096]{2,1,0:T(8,128)(2,1)} %param.14), kind=kOutput, calls=%fused_computation.21 | convolution fusion | flops 201351168 | bytes 25427968 | tf_op jit(solution)/shard_map/dot_general | solution.py:128
  126.9 12.8 %all-reduce = (bf16[8,32]{1,0:T(8,128)(2,1)S(1)}, f32[4,1,2]{2,0,1:T(4,128)}) all-reduce(f32[8,32]{1,0:T(8,128)S(1)} %maximum_multiply_fusion, f32[4,1,2]{2,0,1:T(4,128)S(1)} %all_to_all.38), channel_id=1, replica_groups=mesh['parts'=2,'expert'=4,'tensor'=4] {'tensor'}, use_global_device_ids=true, to_apply=%region_4.5 | all-reduce | flops 264 | bytes 1600 | tf_op jit(solution)/shard_map/psum | solution.py:108
  140.7 4.6 %copy.46 = f32[4,2,3072]{1,0,2:T(4,128)} copy(f32[4,2,3072]{2,1,0:T(2,128)S(1)} %reshape.179) | data formatting | bytes 196608
  145.3 5.8 %reshape.225 = f32[3072,8]{1,0:T(8,128)} reshape(f32[3072,4,2]{2,1,0:T(4,128)} %bitcast.88) | data formatting | bytes 196608
  151.1 3.2 %all-to-all-start.5 = ((f32[4,1,2]{2,1,0:T(1,128)}), f32[4,1,2]{2,1,0:T(1,128)S(1)}, u32[]{:S(2)}, u32[]{:S(2)}) async-start(f32[4,1,2]{2,1,0:T(1,128)} %bitcast.15), calls=%async_computation.5 | async-start | bytes 4096 | tf_op jit(solution)/shard_map/all_to_all | solution.py:143
  155.2 2.9 %all-to-all-done.5 = f32[4,1,2]{2,1,0:T(1,128)S(1)} async-done(((f32[4,1,2]{2,1,0:T(1,128)}), f32[4,1,2]{2,1,0:T(1,128)S(1)}, u32[]{:S(2)}, u32[]{:S(2)}) %all-to-all-start.5) | async-done | bytes 64 | tf_op jit(solution)/shard_map/all_to_all | solution.py:143
  160.2 25.0 %reduce-scatter.4.cloned.1.call-done = f32[768,8]{1,0:T(8,128)} async-done(((f32[3072,8]{1,0:T(8,128)}), f32[768,8]{1,0:T(8,128)}) %reduce-scatter.4.cloned.1.call-update) | async-done | bytes 24592
  185.2 1.7 reshape.226
  188.2 3.3 %all-to-all-start.3 = ((f32[4,2,768]{2,1,0:T(2,128)}), f32[4,2,768]{2,1,0:T(2,128)S(1)}, u32[]{:S(2)}, u32[]{:S(2)}) async-start(f32[4,2,768]{2,1,0:T(2,128)} %copy.47), calls=%async_computation.3 | async-start | bytes 49152 | tf_op jit(solution)/shard_map/all_to_all | solution.py:142
  197.3 3.3 %all-to-all-start.4 = ((f32[4,1,768]{2,1,0:T(1,128)}), f32[4,1,768]{2,1,0:T(1,128)S(1)}, u32[]{:S(2)}, u32[]{:S(2)}) async-start(f32[4,1,768]{2,1,0:T(1,128)} %all_to_all.35), calls=%async_computation.4 | async-start | bytes 24576 | tf_op jit(solution)/shard_map/all_to_all | solution.py:153
  200.5 1.4 fusion.53
  201.9 4.2 %all-to-all-done.4 = f32[4,1,768]{2,1,0:T(1,128)S(1)} async-done(((f32[4,1,768]{2,1,0:T(1,128)}), f32[4,1,768]{2,1,0:T(1,128)S(1)}, u32[]{:S(2)}, u32[]{:S(2)}) %all-to-all-start.4) | async-done | bytes 12320 | tf_op jit(solution)/shard_map/all_to_all | solution.py:153
  (79 shorter events, 19.4 us)
Async XLA Ops:
  7.2 16.4 %copy-start = (bf16[3072,4]{0,1:T(4,128)(2,1)S(1)}, bf16[3072,4]{0,1:T(4,128)(2,1)}, u32[]{:S(2)}) copy-start(bf16[3072,4]{0,1:T(4,128)(2,1)} %param.12) | copy-start | bytes 73732
  24.6 4.3 %copy-start.4 = (f32[4,1]{1,0:T(4,128)}, f32[4,1]{1,0:T(4,128)S(1)}, u32[]{:S(2)}) copy-start(f32[4,1]{1,0:T(4,128)S(1)} %get-tuple-element.10) | copy-start | bytes 52
  25.6 34.2 %all-to-all-start = ((bf16[4,1,2]{2,1,0:T(2,128)(2,1)}), bf16[4,1,2]{2,1,0:T(2,128)(2,1)S(1)}, u32[]{:S(2)}, u32[]{:S(2)}) async-start(bf16[4,1,2]{2,1,0:T(2,128)(2,1)} %convert_element_type.102), calls=%async_computation | async-start | bytes 4096 | tf_op jit(solution)/shard_map/all_to_all | solution.py:67
  59.9 7.3 %all-to-all-start.2 = ((bf16[4,2,3072]{2,1,0:T(2,128)(2,1)}), bf16[4,2,3072]{2,1,0:T(2,128)(2,1)S(1)}, u32[]{:S(2)}, u32[]{:S(2)}) async-start(bf16[4,2,3072]{2,1,0:T(2,128)(2,1)} %reshape.177), calls=%async_computation.2 | async-start | bytes 98304 | tf_op jit(solution)/shard_map/all_to_all | solution.py:53
  67.2 23.0 %all-to-all-start.1 = ((bf16[4,2,3072]{2,1,0:T(2,128)(2,1)}), bf16[4,2,3072]{2,1,0:T(2,128)(2,1)}, u32[]{:S(2)}, u32[]{:S(2)}) async-start(bf16[4,2,3072]{2,1,0:T(2,128)(2,1)} %reshape.175), calls=%async_computation.1 | async-start | bytes 98304 | tf_op jit(solution)/shard_map/all_to_all | solution.py:60
  71.0 114.2 %reduce-scatter.4.cloned.1.call-start = ((), (), s32[]{:S(2)}) async-start(), calls=%async_computation.7 | async-start | bytes 1966080
  71.1 15.3 %copy-start.1 = (bf16[1,3072,4096]{2,1,0:T(8,128)(2,1)S(1)}, bf16[1,3072,4096]{2,1,0:T(8,128)(2,1)}, u32[]{:S(2)}) copy-start(bf16[1,3072,4096]{2,1,0:T(8,128)(2,1)} %param.14) | copy-start | bytes 75497472
  71.3 18.5 %copy-start.2 = (bf16[1,2,16,4096]{3,2,1,0:T(8,128)(2,1)S(1)}, bf16[1,2,16,4096]{3,2,1,0:T(8,128)(2,1)}, u32[]{:S(2)}) copy-start(bf16[1,2,16,4096]{3,2,1,0:T(8,128)(2,1)} %param.17) | copy-start | bytes 786436
  114.4 26.1 %copy-start.3 = (bf16[1,768,32]{1,2,0:T(8,128)(2,1)S(1)}, bf16[1,768,32]{1,2,0:T(8,128)(2,1)}, u32[]{:S(2)}) copy-start(bf16[1,768,32]{1,2,0:T(8,128)(2,1)} %param.16) | copy-start | bytes 147460
  151.1 7.0 %all-to-all-start.5 = ((f32[4,1,2]{2,1,0:T(1,128)}), f32[4,1,2]{2,1,0:T(1,128)S(1)}, u32[]{:S(2)}, u32[]{:S(2)}) async-start(f32[4,1,2]{2,1,0:T(1,128)} %bitcast.15), calls=%async_computation.5 | async-start | bytes 4096 | tf_op jit(solution)/shard_map/all_to_all | solution.py:143
  188.2 7.6 %all-to-all-start.3 = ((f32[4,2,768]{2,1,0:T(2,128)}), f32[4,2,768]{2,1,0:T(2,128)S(1)}, u32[]{:S(2)}, u32[]{:S(2)}) async-start(f32[4,2,768]{2,1,0:T(2,128)} %copy.47), calls=%async_computation.3 | async-start | bytes 49152 | tf_op jit(solution)/shard_map/all_to_all | solution.py:142
  197.3 8.8 %all-to-all-start.4 = ((f32[4,1,768]{2,1,0:T(1,128)}), f32[4,1,768]{2,1,0:T(1,128)S(1)}, u32[]{:S(2)}, u32[]{:S(2)}) async-start(f32[4,1,768]{2,1,0:T(1,128)} %all_to_all.35), calls=%async_computation.4 | async-start | bytes 24576 | tf_op jit(solution)/shard_map/all_to_all | solution.py:153
Sparse Core Ops, SparseCore 0:
  151.2 33.9 reduce-scatter.3
where the time goes:
time: 214 us
  blocking collectives  55 us (26%)
  matrix products  52.5 us (25%)
  waiting for transfers between devices  35.5 us (17%)
  local copies, waits for them, and re-layouts  29.6 us (14%)
  starting transfers between devices  20.2 us (9%)
  between operations  16.8 us (8%)
  other arithmetic  4.04 us (2%)
    unnamed x2, waiting for transfers between devices  25 us
    unnamed x15, local copies, waits for them, and re-layouts  19.2 us
    all_gather x1, blocking collectives, per_device(): lax.all_gather(tokens, 'tensor', axis=0, tiled=True)  14.9 us
    all_gather x1, blocking collectives, per_device(): whole_in = lax.all_gather(adapt_in, 'tensor', axis=0, tiled=True)  13.9 us
    all_gather x1, blocking collectives, per_device(): lax.all_gather(cotangent, 'tensor', axis=0, tiled=True)  13.3 us
    psum x1, blocking collectives, per_device(): lax.psum((latent_share_grad, gate_share), 'tensor')  12.8 us
    dot_general x1, matrix products, per_device(): lax.dot_general(expert_cot, down_mat, contract, preferred_element_type=jn...  11.7 us
    dot_general x1, matrix products, per_device(): lax.dot_general(d_up_pre, up_mat, contract, preferred_element_type=jnp.fl...  11.6 us
  transfers between devices with their start and end apart: 7, of which 4 were waited for; matrix products, arithmetic and copies ran while one was open for 11% of the time, Pallas kernels for 0%

commit v1 on v0

v1 whole, which is shorter than its diff:
```python
import jax
import jax.numpy as jnp
from jax import lax
from jax.experimental import pallas as pl
from jax.experimental.pallas import tpu as pltpu
from jax.sharding import PartitionSpec as P

adapter_scale = 0.5
every_axis = ("parts", "expert", "tensor")
bf16, f32 = jnp.bfloat16, jnp.float32
extra = 128
ahead = 4
vmem = pl.BlockSpec(memory_space=pltpu.VMEM)
hbm = pl.BlockSpec(memory_space=pltpu.HBM)
mib = 2**20


def dot(a, b, a_dim, b_dim):
    return lax.dot_general(a, b, (((a_dim,), (b_dim,)), ((), ())), preferred_element_type=f32)


def in_hbm(array):
    return pltpu.with_memory_space_constraint(array, pltpu.HBM)


def iota(shape, dim):
    return lax.broadcasted_iota(jnp.int32, shape, dim)


def bundle_kernel(tokens_hbm, cotangent_hbm, adapt_hbm, out, rows, sems):
    rank2, cols = adapt_hbm.shape
    copies = [
        pltpu.make_async_copy(tokens_hbm, rows.at[0], sems.at[0]),
        pltpu.make_async_copy(cotangent_hbm, rows.at[1], sems.at[1]),
        pltpu.make_async_copy(adapt_hbm, out.at[:rank2, :], sems.at[2]),
    ]
    for copy in copies:
        copy.start()
    for copy in copies:
        copy.wait()
    cuts = rows.shape[2] // cols
    cut = [
        rows[side, :, k * cols : (k + 1) * cols].astype(f32)
        for side in range(2)
        for k in range(cuts)
    ]
    rest = out.shape[0] - rank2 - 2 * cuts
    if rest:
        cut.append(jnp.zeros((rest, cols), f32))
    out[rank2:, :] = jnp.concatenate(cut, axis=0).astype(bf16)


def pack_kernel(capacity, rank2, *refs):
    routes_hbm, pieces, (out, routes, held, sems) = refs[0], refs[1:-4], refs[-4:]
    count, width = routes_hbm.shape[1], out.shape[2] - extra
    flips = len(pieces) // 2 if len(pieces) == 2 else len(pieces)
    copies = [pltpu.make_async_copy(routes_hbm, routes, sems.at[0])]
    for number, piece in enumerate(pieces):
        source = piece if flips == 1 else piece.at[rank2:, :]
        copies.append(pltpu.make_async_copy(source, held.at[number], sems.at[1 + number]))
    for copy in copies:
        copy.start()
    for copy in copies:
        copy.wait()
    own = lax.axis_index("tensor")
    experts = out.shape[0] // 2
    slots = experts * 2 * capacity
    lane, tail_row = iota((slots, count), 1), iota((count, extra), 0)
    order = jnp.zeros((slots, count), jnp.int32)
    before = jnp.zeros((count, count), jnp.int32)
    after = jnp.zeros((count, count), jnp.int32)
    first = jnp.zeros((slots, count), jnp.int32)
    second = jnp.zeros((slots, count), jnp.int32)
    tail = jnp.zeros((count, extra), jnp.int32)
    tail_lane = iota((count, extra), 1)
    for number in range(count):
        token = lax.bitwise_xor(own, number) if flips > 1 else number
        route0, route1 = routes[0, token], routes[1, token]
        first = jnp.where(lane == number, route0, first)
        second = jnp.where(lane == number, route1, second)
        before = jnp.where(iota((count, count), 0) == number, token, before)
        after = jnp.where(iota((count, count), 1) == number, token, after)
        for place, value in enumerate((route0, route1, 1, token)):
            tail = jnp.where((tail_row == number) & (tail_lane == place), value, tail)
    row = iota((slots, count), 0)
    expert = lax.div(row, 2 * capacity)
    named = (first == expert) | (second == expert)
    earlier = jnp.where(before < after, 1.0, 0.0).astype(bf16)
    position = dot(jnp.where(named, 1.0, 0.0).astype(bf16), earlier, 1, 0)
    placed = named & (position == lax.rem(row, capacity).astype(f32))
    is_token = lax.rem(row, 2 * capacity) < capacity
    take_x = jnp.where(placed & is_token, 1.0, 0.0).astype(bf16)
    take_cot = jnp.where(placed & (~is_token), 1.0, 0.0).astype(bf16)
    if flips == 1:
        x, cot = held[0], held[1]
    else:
        cols = held.shape[2]
        cuts = width // cols
        values = [held[number].astype(f32) for number in range(flips)]

        def uncut(first):
            rows = [
                jnp.concatenate([v[first + k : first + k + 1, :] for k in range(cuts)], axis=1)
                for v in values
            ]
            return jnp.concatenate(rows, axis=0).astype(bf16)

        x, cot = uncut(0), uncut(cuts)
    main = dot(take_x, x, 1, 0) + dot(take_cot, cot, 1, 0)
    tails = dot(take_x, tail.astype(f32).astype(bf16), 1, 0)
    filled = jnp.concatenate([main, tails], axis=1)
    for target in range(2 * experts):
        start = (target % experts) * 2 * capacity
        out[target] = filled[start : start + 2 * capacity, :].astype(bf16)


def spread(rank2, count):
    shape = (rank2, count * rank2)
    return (lax.rem(iota(shape, 1), rank2) == iota(shape, 0)).astype(f32).astype(bf16)


def main_kernel(sizes, *refs):
    tensor_size, expert_size, size_group, capacity, devices, tile = sizes
    (gathered, pieces, refs) = (refs[0], refs[1], refs[2:])
    (router_hbm, out_hbm, gate_hbm, up_hbm, down_hbm, out, sent, kept, own_x, own_latent) = refs[:10]
    (gate_mat, up_mat, down_mat, adapt, router, adapt_out, d_gate, d_up, d_rows, sems, small) = refs[10:]
    part, expert = lax.axis_index("parts"), lax.axis_index("expert")
    width, hidden = gate_mat.shape
    rank2 = adapt.shape[0]
    tiles = hidden // tile
    rows = d_gate.shape[0]
    part_rows = rows // 2
    rank = rank2 // 2

    copies = []
    for step in range(tiles):
        here = pl.ds(step * tile, tile)
        there = pl.ds(pl.multiple_of(part * hidden + step * tile, tile), tile)
        for side, (source, held) in enumerate(
            (
                (gate_hbm.at[0, :, there], gate_mat.at[:, here]),
                (up_hbm.at[0, :, there], up_mat.at[:, here]),
                (down_hbm.at[0, there, :], down_mat.at[here, :]),
            )
        ):
            copies.append(pltpu.make_async_copy(source, held, sems.at[side, step]))
    half_here = pl.ds(pl.multiple_of(part * hidden, hidden), hidden)
    minor = [
        pltpu.make_async_copy(router_hbm, router, small.at[0]),
        pltpu.make_async_copy(out_hbm.at[:, :, half_here], adapt_out, small.at[1]),
    ]
    if len(pieces) == 1:
        minor.append(pltpu.make_async_copy(pieces[0], adapt, small.at[2]))
    else:
        own = lax.axis_index("tensor")
        cols = pieces[0].shape[1]
        for flip, piece in enumerate(pieces):
            first = pl.multiple_of(lax.bitwise_xor(own, flip) * cols, cols)
            minor.append(
                pltpu.make_async_copy(
                    piece.at[:rank2, :], adapt.at[:, pl.ds(first, cols)], small.at[2 + flip]
                )
            )
    for copy in minor + copies[:ahead]:
        copy.start()

    def arrived(number):
        copies[number].wait()
        if number + ahead < len(copies):
            copies[number + ahead].start()

    sources = gathered.shape[0]
    slot_x = jnp.concatenate(
        [gathered[k, :capacity, :].astype(f32) for k in range(sources)], axis=0
    )
    x = slot_x[:, :width].astype(bf16)
    cot = jnp.concatenate(
        [gathered[k, capacity:, :width].astype(f32) for k in range(sources)], axis=0
    ).astype(bf16)
    route0 = slot_x[:, width : width + 1]
    route1 = slot_x[:, width + 1 : width + 2]
    used = slot_x[:, width + 2 : width + 3]
    token = slot_x[:, width + 3 : width + 4]
    expert_f = expert.astype(f32)
    group = lax.div(iota((rows, devices), 0), capacity) * size_group
    dispatch = ((iota((rows, devices), 1) - group).astype(f32) == token) & (used > 0.5)
    dispatch = jnp.where(dispatch, 1.0, 0.0).astype(bf16)
    for copy in minor:
        copy.wait()

    logits = dot(x, router[...], 1, 1)
    ids = iota(logits.shape, 1).astype(f32)
    signs = jnp.where(ids == route0, 1.0, 0.0) - jnp.where(ids == route1, 1.0, 0.0)
    chance = jax.nn.sigmoid(jnp.sum(signs * logits, axis=1, keepdims=True))
    is_first = route0 == expert_f
    gate = jnp.where(is_first, chance, 1.0 - chance).astype(bf16).astype(f32) * used
    slope = jnp.where(is_first, 1.0, -1.0) * used * chance * (1.0 - chance)

    latent = dot(x, adapt[...], 1, 1).astype(bf16)
    latent_gate, latent_up = latent[:, :rank], latent[:, rank:]

    gate_share = jnp.zeros((rows, 1), f32)
    share_gate = jnp.zeros((rows, rank), f32)
    share_up = jnp.zeros((rows, rank), f32)
    for step in range(tiles):
        here = pl.ds(step * tile, tile)
        gate_out = adapt_out[0, :, here]
        up_out = adapt_out[1, :, here]
        gate_val = adapter_scale * dot(latent_gate, gate_out, 1, 0)
        up_val = adapter_scale * dot(latent_up, up_out, 1, 0)
        arrived(3 * step)
        gate_val = gate_val + dot(x, gate_mat[:, here], 1, 0)
        arrived(3 * step + 1)
        up_val = up_val + dot(x, up_mat[:, here], 1, 0)
        arrived(3 * step + 2)
        returned = dot(cot, down_mat[here, :], 1, 1)
        sig = jax.nn.sigmoid(gate_val)
        activated = gate_val * sig
        gate_share = gate_share + jnp.sum(returned * (activated * up_val), axis=1, keepdims=True)
        d_hidden = gate * returned
        d_gate_tile = (d_hidden * up_val * sig * (1.0 + gate_val * (1.0 - sig))).astype(bf16)
        d_up_tile = (d_hidden * activated).astype(bf16)
        d_gate[:, here] = d_gate_tile
        d_up[:, here] = d_up_tile
        share_gate = share_gate + dot(d_gate_tile, gate_out, 1, 1)
        share_up = share_up + dot(d_up_tile, up_out, 1, 1)
        added = dot(d_gate_tile, gate_mat[:, here], 1, 1) + dot(d_up_tile, up_mat[:, here], 1, 1)
        if step == 0:
            d_rows[...] = added
        else:
            d_rows[...] += added
    share = adapter_scale * jnp.concatenate([share_gate, share_up], axis=1)

    high = share.astype(bf16)
    low = (share - high.astype(f32)).astype(bf16)
    all_rows = d_rows[...] + dot(high, adapt[...], 1, 0) + dot(low, adapt[...], 1, 0)
    all_rows = all_rows + (gate_share * slope) * dot(signs.astype(bf16), router[...], 1, 0)

    token_grads = dot(dispatch, all_rows.astype(bf16), 0, 0).astype(bf16)
    lanes = part_rows * rank2
    flat = dot(high, spread(rank2, part_rows), 1, 0)
    mine = lax.div(iota((rows, lanes), 1), rank2) == lax.rem(iota((rows, lanes), 0), part_rows)
    flat = jnp.where(mine, flat, 0.0).astype(bf16)
    target, source = iota((devices, rows), 0), iota((devices, rows), 1)
    to_expert = lax.rem(lax.div(target, tensor_size), expert_size) == expert
    to_part = lax.div(target, tensor_size * expert_size) == lax.div(source, part_rows)
    goes = jnp.where(to_expert & to_part, 1.0, 0.0).astype(bf16)
    latent_grads = dot(goes, flat, 1, 0).astype(bf16)
    half, half_lanes = width // 2, lanes // 2
    out[:, 0, :] = jnp.concatenate([token_grads[:, :half], latent_grads[:, :half_lanes]], axis=1)
    out[:, 1, :] = jnp.concatenate([token_grads[:, half:], latent_grads[:, half_lanes:]], axis=1)

    def of_part(array, own):
        top, bottom = array[:part_rows, :], array[part_rows:, :]
        return jnp.where((part == 0) == own, top, bottom)

    d_gate_all, d_up_all = d_gate[...].astype(f32), d_up[...].astype(f32)
    for ref, own in ((sent, False), (kept, True)):
        ref[...] = jnp.concatenate([of_part(d_gate_all, own), of_part(d_up_all, own)], 0).astype(bf16)
    own_x[...] = of_part(x.astype(f32), True).astype(bf16)
    own_latent[...] = of_part(latent.astype(f32), True).astype(bf16)


def up_kernel(kept, received, latent, out):
    part = lax.axis_index("parts")
    rows, rank2 = latent.shape
    hidden = kept.shape[1]
    rank = rank2 // 2
    for ref, number in ((kept, part), (received, 1 - part)):
        cols = pl.ds(pl.multiple_of(number * hidden, hidden), hidden)
        for side in range(2):
            out[side, :, cols] = adapter_scale * dot(
                latent[:, side * rank : (side + 1) * rank],
                ref[side * rows : (side + 1) * rows, :],
                0,
                0,
            )


def last_kernel(received, x_cols, grad_tokens, grad_down):
    rank2, cols = grad_down.shape
    width = grad_tokens.shape[1]
    half = width // 2
    if x_cols.shape[1] == cols:
        x = x_cols[...]
    else:
        x = x_cols[:, pl.ds(pl.multiple_of(lax.axis_index("tensor") * cols, cols), cols)]
    rows = x.shape[0]
    total = jnp.sum(received[...].astype(f32), axis=0)
    grad_tokens[...] = jnp.concatenate([total[0:1, :half], total[1:2, :half]], axis=1).astype(bf16)
    flat = jnp.concatenate([total[0:1, half:], total[1:2, half:]], axis=1)
    lanes = rows * rank2
    mine = lax.div(iota((rows, lanes), 1), rank2) == iota((rows, lanes), 0)
    d_latent = dot(jnp.where(mine, flat, 0.0).astype(bf16), spread(rank2, rows), 1, 1).astype(bf16)
    grad_down[...] = dot(d_latent, x, 0, 0)


def per_device(tokens, cotangent, routes, router, w_gate, w_up, w_down, adapter_down, adapter_up):
    parts, expert_size = lax.axis_size("parts"), lax.axis_size("expert")
    tensor_size = lax.axis_size("tensor")
    devices = parts * expert_size * tensor_size
    size_group, experts = routes.shape[0], router.shape[1]
    capacity = 2 * size_group // experts * 5 // 4
    width = tokens.shape[1]
    hidden = w_gate.shape[2] // parts
    rank2 = adapter_down.shape[2]
    col_width = adapter_down.shape[1]
    part_rows = expert_size * capacity
    rows = parts * part_rows
    tile = min(hidden, 512)
    tiles = hidden // tile
    lanes = part_rows * rank2

    adapt_in = adapter_down[0].T
    by_flip = tensor_size == 4 and col_width % 128 == 0

    if by_flip:
        cuts = width // col_width
        bundle_rows = rank2 + -(-2 * cuts // 16) * 16
        bundle = pl.pallas_call(
            bundle_kernel,
            out_shape=jax.ShapeDtypeStruct((bundle_rows, col_width), bf16),
            in_specs=[hbm] * 3,
            out_specs=vmem,
            scratch_shapes=[pltpu.VMEM((2, 1, width), bf16), pltpu.SemaphoreType.DMA((3,))],
            compiler_params=pltpu.CompilerParams(vmem_limit_bytes=2 * mib),
            name="bundle",
        )(in_hbm(tokens), in_hbm(cotangent), in_hbm(adapt_in))
        pieces = [bundle] + [
            lax.ppermute(bundle, "tensor", [(i, i ^ flip) for i in range(tensor_size)])
            for flip in range(1, tensor_size)
        ]
        group_rows = pieces
        held = (len(pieces), bundle_rows - rank2, col_width)
    else:
        pieces = [lax.all_gather(adapt_in, "tensor", axis=1, tiled=True)]
        group_rows = [
            lax.all_gather(rows, "tensor", axis=0, tiled=True) for rows in (tokens, cotangent)
        ]
        held = (2, size_group, width)
    packed = pl.pallas_call(
        lambda *refs: pack_kernel(capacity, rank2, *refs),
        out_shape=jax.ShapeDtypeStruct((parts * experts, 2 * capacity, width + extra), bf16),
        in_specs=[hbm] * (1 + len(group_rows)),
        out_specs=vmem,
        scratch_shapes=[
            pltpu.SMEM(routes.shape[::-1], jnp.int32),
            pltpu.VMEM(held, bf16),
            pltpu.SemaphoreType.DMA((1 + len(group_rows),)),
        ],
        compiler_params=pltpu.CompilerParams(vmem_limit_bytes=32 * mib),
        name="pack",
    )(in_hbm(routes.T), *[in_hbm(piece) for piece in group_rows])
    gathered = lax.all_to_all(packed, ("parts", "expert"), split_axis=0, concat_axis=0, tiled=True)

    sizes = (tensor_size, expert_size, size_group, capacity, devices, tile)

    def main(*refs):
        main_kernel(sizes, refs[0], refs[1 : 1 + len(pieces)], *refs[1 + len(pieces) :])

    out, sent, kept, own_x, own_latent = pl.pallas_call(
        main,
        out_shape=(
            jax.ShapeDtypeStruct((devices, 2, (width + lanes) // 2), bf16),
            jax.ShapeDtypeStruct((2 * part_rows, hidden), bf16),
            jax.ShapeDtypeStruct((2 * part_rows, hidden), bf16),
            jax.ShapeDtypeStruct((part_rows, width), bf16),
            jax.ShapeDtypeStruct((part_rows, rank2), bf16),
        ),
        in_specs=[vmem] + [hbm] * (len(pieces) + 5),
        out_specs=[vmem] * 5,
        scratch_shapes=[
            pltpu.VMEM((width, hidden), bf16),
            pltpu.VMEM((width, hidden), bf16),
            pltpu.VMEM((hidden, width), bf16),
            pltpu.VMEM((rank2, width), bf16),
            pltpu.VMEM((experts, width), bf16),
            pltpu.VMEM((2, rank2 // 2, hidden), bf16),
            pltpu.VMEM((rows, hidden), bf16),
            pltpu.VMEM((rows, hidden), bf16),
            pltpu.VMEM((rows, width), f32),
            pltpu.SemaphoreType.DMA((3, tiles)),
            pltpu.SemaphoreType.DMA((2 + len(pieces),)),
        ],
        cost_estimate=pl.CostEstimate(
            flops=10 * rows * width * hidden,
            bytes_accessed=6 * width * hidden,
            transcendentals=rows * hidden,
        ),
        compiler_params=pltpu.CompilerParams(vmem_limit_bytes=50 * mib),
        name="main",
    )(
        gathered,
        *[in_hbm(piece) for piece in pieces],
        in_hbm(router.T),
        in_hbm(adapter_up[0]),
        in_hbm(w_gate),
        in_hbm(w_up),
        in_hbm(w_down),
    )

    received = lax.all_to_all(out, every_axis, split_axis=0, concat_axis=0, tiled=True)
    other = lax.ppermute(sent, "parts", [(0, 1), (1, 0)])
    grad_up = pl.pallas_call(
        up_kernel,
        out_shape=jax.ShapeDtypeStruct(adapter_up.shape[1:], f32),
        in_specs=[vmem] * 3,
        out_specs=vmem,
        cost_estimate=pl.CostEstimate(
            flops=8 * part_rows * rank2 * hidden,
            bytes_accessed=8 * rank2 * hidden,
            transcendentals=0,
        ),
        compiler_params=pltpu.CompilerParams(vmem_limit_bytes=16 * mib),
        name="grad_up",
    )(kept, other, own_latent)

    if col_width % 128 == 0:
        x_cols = own_x
    else:
        x_cols = lax.dynamic_slice_in_dim(
            own_x, lax.axis_index("tensor") * col_width, col_width, 1
        )
    grad_tokens, grad_down = pl.pallas_call(
        last_kernel,
        out_shape=(
            jax.ShapeDtypeStruct(tokens.shape, bf16),
            jax.ShapeDtypeStruct((rank2, col_width), f32),
        ),
        in_specs=[vmem] * 2,
        out_specs=[vmem] * 2,
        compiler_params=pltpu.CompilerParams(vmem_limit_bytes=40 * mib),
        name="last",
    )(received, x_cols)
    return (grad_tokens, grad_down.T[None], grad_up[None])


def solution(mesh):
    return jax.shard_map(
        per_device,
        mesh=mesh,
        in_specs=(
            P(every_axis, None),
            P(every_axis, None),
            P(("parts", "expert"), None),
            P(),
            P("expert", None, "tensor"),
            P("expert", None, "tensor"),
            P("expert", "tensor", None),
            P("expert", "tensor", None),
            P("expert", None, None, "tensor"),
        ),
        out_specs=(
            P(every_axis, None),
            P(("parts", "expert"), "tensor", None),
            P(("parts", "expert"), None, None, "tensor"),
        ),
        check_vma=False,
    )
```

time: 214 us -> 58.7 us (0.27)
  matrix products: 52.5 us -> 0 us
  blocking collectives: 55 us -> 9.84 us
  local copies, waits for them, and re-layouts: 29.6 us -> 0.65 us
  Pallas kernels: 0 us -> 24.3 us
  waiting for transfers between devices: 35.5 us -> 12.2 us
  between operations: 16.8 us -> 0.69 us
  starting transfers between devices: 20.2 us -> 10.7 us
  other arithmetic: 4.04 us -> 0 us
    dot_general x18 -> x0, matrix products: 52.5 us -> none  [the longest x1 11.7 us: per_device(): lax.dot_general(expert_cot, down_mat, contract, preferred_element_type=jn...]
    all_gather x3 -> x0, blocking collectives: 42.2 us -> none  [the longest x1 14.9 us: per_device(): lax.all_gather(tokens, 'tensor', axis=0, tiled=True)]
    unnamed x2 -> x0, waiting for transfers between devices: 25 us -> none
    pallas_call x0 -> x5, Pallas kernels: none -> 24.3 us  [the longest x1 20.1 us: per_device(): pl.pallas_call(main, out_shape=(jax.ShapeDtypeStruct((devices, 2, (width...]
    unnamed x15 -> x8, local copies, waits for them, and re-layouts: 19.2 us -> 0.65 us
    all_to_all x6 -> x1, starting transfers between devices: 20.1 us -> 3.09 us  [per_device(): lax.all_to_all(out, every_axis, split_axis=0, concat_axis=0, tiled=True)]
    psum x1 -> x0, blocking collectives: 12.8 us -> none  [per_device(): lax.psum((latent_share_grad, gate_share), 'tensor')]
    all_to_all x0 -> x1, blocking collectives: none -> 9.84 us  [per_device(): lax.all_to_all(packed, ('parts', 'expert'), split_axis=0, concat_axis=0,...]
  transfers between devices with their start and end apart: 7 -> 5, of which waited for: 4 -> 4; matrix products, arithmetic and copies ran while one was open for 11% -> 0% of each run, Pallas kernels for 0% -> 2%
where the time goes in v1:
time: 58.7 us; the launch traced here: 58.3 us
  Pallas kernels  24.3 us (41%)
  waiting for transfers between devices  12.2 us (21%)
  starting transfers between devices  10.7 us (18%)
  blocking collectives  9.84 us (17%)
  between operations  0.69 us (1%)
  local copies, waits for them, and re-layouts  0.65 us (1%)
    pallas_call x1, Pallas kernels, per_device(): pl.pallas_call(main, out_shape=(jax.ShapeDtypeStruct((devices, 2, (width...  20.1 us
    all_to_all x1, blocking collectives, per_device(): lax.all_to_all(packed, ('parts', 'expert'), split_axis=0, concat_axis=0,...  9.84 us
    ppermute x3, starting transfers between devices, per_device(): lax.ppermute(bundle, 'tensor', [(i, i ^ flip) for i in range(tensor_size)])  5.76 us
    ppermute x3, waiting for transfers between devices, per_device(): lax.ppermute(bundle, 'tensor', [(i, i ^ flip) for i in range(tensor_size)])  5.57 us
    ppermute x1, waiting for transfers between devices, per_device(): other = lax.ppermute(sent, 'parts', [(0, 1), (1, 0)])  3.61 us
    all_to_all x1, starting transfers between devices, per_device(): lax.all_to_all(out, every_axis, split_axis=0, concat_axis=0, tiled=True)  3.09 us
    all_to_all x1, waiting for transfers between devices, per_device(): lax.all_to_all(out, every_axis, split_axis=0, concat_axis=0, tiled=True)  3.03 us
    ppermute x1, starting transfers between devices, per_device(): other = lax.ppermute(sent, 'parts', [(0, 1), (1, 0)])  1.83 us
  transfers between devices with their start and end apart: 5, of which 4 were waited for; matrix products, arithmetic and copies ran while one was open for 0% of the time, Pallas kernels for 2%

profile of v1, /device:TPU:0, one launch (start us, length us, event | category | flops | bytes accessed | tf_op | source)
XLA Modules:
  0.0 58.3 jit_solution(16373317621256840754)
XLA Ops:
  0.6 0.9 %bundle.1.refs_1_ = bf16[48,768]{1,0:T(8,128)(2,1)S(1)} custom-call(bf16[1,3072]{1,0:T(2,128)(2,1)} %tokens_hbm.1, bf16[1,3072]{1,0:T(2,128)(2,1)} %cotangent_hbm.1, bf16[32,768]{1,0:T(8,128)(2,1)} %bitcast.12), custom_call_target="tpu_custom_call" | custom-call | tf_op jit(solution)/shard_map/bundle/pallas_call | solution.py:320
  1.5 0.0 copy-start
  1.5 5.1 %collective-permute-start.2 = (bf16[48,768]{1,0:T(8,128)(2,1)S(1)}, bf16[48,768]{1,0:T(8,128)(2,1)S(1)}, u32[]{:S(2)}, u32[]{:S(2)}) collective-permute-start(bf16[48,768]{1,0:T(8,128)(2,1)S(1)} %bundle.1.refs_1_), channel_id=1, source_target_pairs={{0,3},{1,2},{2,1},{3,0},{4,7},{5,6},{6,5},{7,4},{8,11},{9,10},{10,... | collective-permute-start | bytes 221192 | tf_op jit(solution)/shard_map/ppermute | solution.py:330
  6.6 0.0 collective-permute-start.1
  6.6 0.6 %collective-permute-start = (bf16[48,768]{1,0:T(8,128)(2,1)S(1)}, bf16[48,768]{1,0:T(8,128)(2,1)S(1)}, u32[]{:S(2)}, u32[]{:S(2)}) collective-permute-start(bf16[48,768]{1,0:T(8,128)(2,1)S(1)} %bundle.1.refs_1_), channel_id=1, source_target_pairs={{0,1},{1,0},{2,3},{3,2},{4,5},{5,4},{6,7},{7,6},{8,9},{9,8},{10,11... | collective-permute-start | bytes 221192 | tf_op jit(solution)/shard_map/ppermute | solution.py:330
  7.3 2.1 %collective-permute-done.2.refs_4_ = bf16[48,768]{1,0:T(8,128)(2,1)S(1)} collective-permute-done((bf16[48,768]{1,0:T(8,128)(2,1)S(1)}, bf16[48,768]{1,0:T(8,128)(2,1)S(1)}, u32[]{:S(2)}, u32[]{:S(2)}) %collective-permute-start.2) | collective-permute-done | bytes 73760 | tf_op jit(solution)/shard_map/ppermute | solution.py:330
  9.4 0.0 copy-start.1
  9.4 3.5 %collective-permute-done.1.refs_3_ = bf16[48,768]{1,0:T(8,128)(2,1)S(1)} collective-permute-done((bf16[48,768]{1,0:T(8,128)(2,1)S(1)}, bf16[48,768]{1,0:T(8,128)(2,1)S(1)}, u32[]{:S(2)}, u32[]{:S(2)}) %collective-permute-start.1) | collective-permute-done | bytes 73760 | tf_op jit(solution)/shard_map/ppermute | solution.py:330
  12.9 0.0 copy-start.2
  12.9 0.0 collective-permute-done.refs_2_
  12.9 0.0 copy-start.3
  12.9 0.0 copy-done
  12.9 0.0 copy-done.1
  12.9 0.6 %copy-done.2 = bf16[48,768]{1,0:T(8,128)(2,1)} copy-done((bf16[48,768]{1,0:T(8,128)(2,1)}, bf16[48,768]{1,0:T(8,128)(2,1)S(1)}, u32[]{:S(2)}) %copy-start.2) | copy-done | bytes 73752
  13.5 0.0 copy-done.3
  13.5 1.2 %pack.1 = bf16[8,4,3200]{2,1,0:T(4,128)(2,1)S(1)} custom-call(s32[2,4]{1,0:T(2,128)} %bitcast.14, bf16[48,768]{1,0:T(8,128)(2,1)} %copy-done, bf16[48,768]{1,0:T(8,128)(2,1)} %copy-done.3, bf16[48,768]{1,0:T(8,128)(2,1)} %copy-done.2, bf16[48,768]{1,0:T(8,128)(2,1)} %copy-done.1), custom_call_target="tpu_custom_call" | custom-call | tf_op jit(solution)/shard_map/pack/pallas_call | solution.py:341
  14.7 9.8 %all_to_all.10.refs_0_ = bf16[8,4,3200]{2,1,0:T(4,128)(2,1)S(1)} all-to-all(bf16[8,4,3200]{2,1,0:T(4,128)(2,1)S(1)} %pack.1), channel_id=1, replica_groups=mesh['parts'=2,'expert'=4,'tensor'=4] {'parts','expert'}, dimensions={0} | all-to-all | bytes 409600 | tf_op jit(solution)/shard_map/all_to_all | solution.py:354
  24.5 20.1 %main.1 = (bf16[32,2,1664]{2,1,0:T(2,128)(2,1)}, bf16[16,2048]{1,0:T(8,128)(2,1)S(1)}, bf16[16,2048]{1,0:T(8,128)(2,1)S(1)}, bf16[8,3072]{1,0:T(8,128)(2,1)S(1)}, bf16[8,32]{1,0:T(8,128)(2,1)S(1)}) custom-call(bf16[8,4,3200]{2,1,0:T(4,128)(2,1)S(1)} %all_to_all.10.refs_0_, bf16[48,768]{1,0:T(8,128)(2,1)} %copy-done, bf16[48,768]{1,0:T(8,128)(2,1)} %copy-done.3, ...), custom_call_target="tpu_custom_call" | custom-call | flops 1006632960 | bytes 37748736 | tf_op jit(solution)/shard_map/main/pallas_call | solution.py:361
  44.6 3.1 %all-to-all-start.1 = ((bf16[32,2,1664]{2,1,0:T(2,128)(2,1)}), bf16[32,2,1664]{2,1,0:T(2,128)(2,1)S(1)}, u32[]{:S(2)}, u32[]{:S(2)}) async-start(bf16[32,2,1664]{2,1,0:T(2,128)(2,1)} %get-tuple-element.10), calls=%async_computation.1 | async-start | bytes 425984 | tf_op jit(solution)/shard_map/all_to_all | solution.py:402
  47.7 1.8 %collective-permute-start.3 = (bf16[16,2048]{1,0:T(8,128)(2,1)S(1)}, bf16[16,2048]{1,0:T(8,128)(2,1)S(1)}, u32[]{:S(2)}, u32[]{:S(2)}) collective-permute-start(bf16[16,2048]{1,0:T(8,128)(2,1)S(1)} %get-tuple-element.15), channel_id=1, source_target_pairs={{0,16},{16,0},{1,17},{17,1},{2,18},{18,2},{3,19},{19,3},{4,20},{20... | collective-permute-start | bytes 196616 | tf_op jit(solution)/shard_map/ppermute | solution.py:403
  49.6 3.6 %collective-permute-done.3.received = bf16[16,2048]{1,0:T(8,128)(2,1)S(1)} collective-permute-done((bf16[16,2048]{1,0:T(8,128)(2,1)S(1)}, bf16[16,2048]{1,0:T(8,128)(2,1)S(1)}, u32[]{:S(2)}, u32[]{:S(2)}) %collective-permute-start.3) | collective-permute-done | bytes 65568 | tf_op jit(solution)/shard_map/ppermute | solution.py:403
  53.2 1.1 %grad_up.1 = f32[2,16,4096]{2,1,0:T(8,128)} custom-call(bf16[16,2048]{1,0:T(8,128)(2,1)S(1)} %get-tuple-element.14.kept, bf16[16,2048]{1,0:T(8,128)(2,1)S(1)} %collective-permute-done.3.received, bf16[8,32]{1,0:T(8,128)(2,1)S(1)} %get-tuple-element.16.latent), custom_call_target="tpu_custom_call" | custom-call | flops 4194304 | bytes 524288 | tf_op jit(solution)/shard_map/grad_up/pallas_call | solution.py:404
  54.3 3.0 %all-to-all-done.1.received = bf16[32,2,1664]{2,1,0:T(2,128)(2,1)S(1)} async-done(((bf16[32,2,1664]{2,1,0:T(2,128)(2,1)}), bf16[32,2,1664]{2,1,0:T(2,128)(2,1)S(1)}, u32[]{:S(2)}, u32[]{:S(2)}) %all-to-all-start.1) | async-done | bytes 213024 | tf_op jit(solution)/shard_map/all_to_all | solution.py:402
  57.3 1.0 %last.1 = (bf16[1,3072]{1,0:T(2,128)(2,1)}, f32[32,768]{1,0:T(8,128)}) custom-call(bf16[32,2,1664]{2,1,0:T(2,128)(2,1)S(1)} %all-to-all-done.1.received, bf16[8,3072]{1,0:T(8,128)(2,1)S(1)} %get-tuple-element.11.x_cols), custom_call_target="tpu_custom_call" | custom-call | tf_op jit(solution)/shard_map/last/pallas_call | solution.py:424
Async XLA Ops:
  1.5 11.4 %copy-start = (bf16[48,768]{1,0:T(8,128)(2,1)}, bf16[48,768]{1,0:T(8,128)(2,1)S(1)}, u32[]{:S(2)}) copy-start(bf16[48,768]{1,0:T(8,128)(2,1)S(1)} %bundle.1.refs_1_) | copy-start | bytes 221188
  1.5 7.9 %collective-permute-start.2 = (bf16[48,768]{1,0:T(8,128)(2,1)S(1)}, bf16[48,768]{1,0:T(8,128)(2,1)S(1)}, u32[]{:S(2)}, u32[]{:S(2)}) collective-permute-start(bf16[48,768]{1,0:T(8,128)(2,1)S(1)} %bundle.1.refs_1_), channel_id=1, source_target_pairs={{0,3},{1,2},{2,1},{3,0},{4,7},{5,6},{6,5},{7,4},{8,11},{9,10},{10,... | collective-permute-start | bytes 221192 | tf_op jit(solution)/shard_map/ppermute | solution.py:330
  6.6 6.2 %collective-permute-start.1 = (bf16[48,768]{1,0:T(8,128)(2,1)S(1)}, bf16[48,768]{1,0:T(8,128)(2,1)S(1)}, u32[]{:S(2)}, u32[]{:S(2)}) collective-permute-start(bf16[48,768]{1,0:T(8,128)(2,1)S(1)} %bundle.1.refs_1_), channel_id=1, source_target_pairs={{0,2},{1,3},{2,0},{3,1},{4,6},{5,7},{6,4},{7,5},{8,10},{9,11},{10,... | collective-permute-start | bytes 221192 | tf_op jit(solution)/shard_map/ppermute | solution.py:330
  6.6 6.2 %collective-permute-start = (bf16[48,768]{1,0:T(8,128)(2,1)S(1)}, bf16[48,768]{1,0:T(8,128)(2,1)S(1)}, u32[]{:S(2)}, u32[]{:S(2)}) collective-permute-start(bf16[48,768]{1,0:T(8,128)(2,1)S(1)} %bundle.1.refs_1_), channel_id=1, source_target_pairs={{0,1},{1,0},{2,3},{3,2},{4,5},{5,4},{6,7},{7,6},{8,9},{9,8},{10,11... | collective-permute-start | bytes 221192 | tf_op jit(solution)/shard_map/ppermute | solution.py:330
  9.4 3.5 %copy-start.1 = (bf16[48,768]{1,0:T(8,128)(2,1)}, bf16[48,768]{1,0:T(8,128)(2,1)S(1)}, u32[]{:S(2)}) copy-start(bf16[48,768]{1,0:T(8,128)(2,1)S(1)} %collective-permute-done.2.refs_4_) | copy-start | bytes 221188
  12.9 0.6 %copy-start.2 = (bf16[48,768]{1,0:T(8,128)(2,1)}, bf16[48,768]{1,0:T(8,128)(2,1)S(1)}, u32[]{:S(2)}) copy-start(bf16[48,768]{1,0:T(8,128)(2,1)S(1)} %collective-permute-done.1.refs_3_) | copy-start | bytes 221188
  12.9 0.7 %copy-start.3 = (bf16[48,768]{1,0:T(8,128)(2,1)}, bf16[48,768]{1,0:T(8,128)(2,1)S(1)}, u32[]{:S(2)}) copy-start(bf16[48,768]{1,0:T(8,128)(2,1)S(1)} %collective-permute-done.refs_2_) | copy-start | bytes 221188
  44.6 12.7 %all-to-all-start.1 = ((bf16[32,2,1664]{2,1,0:T(2,128)(2,1)}), bf16[32,2,1664]{2,1,0:T(2,128)(2,1)S(1)}, u32[]{:S(2)}, u32[]{:S(2)}) async-start(bf16[32,2,1664]{2,1,0:T(2,128)(2,1)} %get-tuple-element.10), calls=%async_computation.1 | async-start | bytes 425984 | tf_op jit(solution)/shard_map/all_to_all | solution.py:402
  47.7 5.4 %collective-permute-start.3 = (bf16[16,2048]{1,0:T(8,128)(2,1)S(1)}, bf16[16,2048]{1,0:T(8,128)(2,1)S(1)}, u32[]{:S(2)}, u32[]{:S(2)}) collective-permute-start(bf16[16,2048]{1,0:T(8,128)(2,1)S(1)} %get-tuple-element.15), channel_id=1, source_target_pairs={{0,16},{16,0},{1,17},{17,1},{2,18},{18,2},{3,19},{19,3},{4,20},{20... | collective-permute-start | bytes 196616 | tf_op jit(solution)/shard_map/ppermute | solution.py:403

commit v2 on v1

--- a/solution.py
+++ b/solution.py
@@ -9,7 +9,7 @@
 every_axis = ("parts", "expert", "tensor")
 bf16, f32 = jnp.bfloat16, jnp.float32
 extra = 128
-ahead = 4
+ahead = 2
 vmem = pl.BlockSpec(memory_space=pltpu.VMEM)
 hbm = pl.BlockSpec(memory_space=pltpu.HBM)
 mib = 2**20
@@ -50,23 +50,35 @@
     out[rank2:, :] = jnp.concatenate(cut, axis=0).astype(bf16)
 
 
-def pack_kernel(capacity, rank2, *refs):
-    routes_hbm, pieces, (out, routes, held, sems) = refs[0], refs[1:-4], refs[-4:]
-    count, width = routes_hbm.shape[1], out.shape[2] - extra
-    flips = len(pieces) // 2 if len(pieces) == 2 else len(pieces)
-    copies = [pltpu.make_async_copy(routes_hbm, routes, sems.at[0])]
-    for number, piece in enumerate(pieces):
-        source = piece if flips == 1 else piece.at[rank2:, :]
-        copies.append(pltpu.make_async_copy(source, held.at[number], sems.at[1 + number]))
-    for copy in copies:
-        copy.start()
-    for copy in copies:
-        copy.wait()
+def pack_kernel(capacity, rank2, flips, routes_hbm, *refs):
+    pieces, (outs, adapt, routes, sem) = refs[:-4], refs[-4:]
+    count, width = routes_hbm.shape[1], adapt.shape[1]
+    copy = pltpu.make_async_copy(routes_hbm, routes, sem)
+    copy.start()
     own = lax.axis_index("tensor")
-    experts = out.shape[0] // 2
+    if flips == 1:
+        x, cot = pieces[0][...], pieces[1][...]
+        adapt[...] = pieces[2][...]
+    else:
+        cols = pieces[0].shape[1]
+        cuts = width // cols
+        values = [piece[rank2:, :].astype(f32) for piece in pieces]
+
+        def uncut(first):
+            rows = [
+                jnp.concatenate([v[first + k : first + k + 1, :] for k in range(cuts)], axis=1)
+                for v in values
+            ]
+            return jnp.concatenate(rows, axis=0).astype(bf16)
+
+        x, cot = uncut(0), uncut(cuts)
+        for flip, piece in enumerate(pieces):
+            first = pl.multiple_of(lax.bitwise_xor(own, flip) * cols, cols)
+            adapt[:, pl.ds(first, cols)] = piece[:rank2, :]
+    copy.wait()
+    experts = len(outs)
     slots = experts * 2 * capacity
     lane, tail_row = iota((slots, count), 1), iota((count, extra), 0)
-    order = jnp.zeros((slots, count), jnp.int32)
     before = jnp.zeros((count, count), jnp.int32)
     after = jnp.zeros((count, count), jnp.int32)
     first = jnp.zeros((slots, count), jnp.int32)
@@ -83,7 +95,7 @@
         for place, value in enumerate((route0, route1, 1, token)):
             tail = jnp.where((tail_row == number) & (tail_lane == place), value, tail)
     row = iota((slots, count), 0)
-    expert = lax.div(row, 2 * capacity)
+    expert = lax.bitwise_xor(lax.div(row, 2 * capacity), lax.axis_index("expert"))
     named = (first == expert) | (second == expert)
     earlier = jnp.where(before < after, 1.0, 0.0).astype(bf16)
     position = dot(jnp.where(named, 1.0, 0.0).astype(bf16), earlier, 1, 0)
@@ -91,27 +103,36 @@
     is_token = lax.rem(row, 2 * capacity) < capacity
     take_x = jnp.where(placed & is_token, 1.0, 0.0).astype(bf16)
     take_cot = jnp.where(placed & (~is_token), 1.0, 0.0).astype(bf16)
-    if flips == 1:
-        x, cot = held[0], held[1]
-    else:
-        cols = held.shape[2]
-        cuts = width // cols
-        values = [held[number].astype(f32) for number in range(flips)]
-
-        def uncut(first):
-            rows = [
-                jnp.concatenate([v[first + k : first + k + 1, :] for k in range(cuts)], axis=1)
-                for v in values
-            ]
-            return jnp.concatenate(rows, axis=0).astype(bf16)
-
-        x, cot = uncut(0), uncut(cuts)
     main = dot(take_x, x, 1, 0) + dot(take_cot, cot, 1, 0)
     tails = dot(take_x, tail.astype(f32).astype(bf16), 1, 0)
     filled = jnp.concatenate([main, tails], axis=1)
-    for target in range(2 * experts):
-        start = (target % experts) * 2 * capacity
-        out[target] = filled[start : start + 2 * capacity, :].astype(bf16)
+    for number, out in enumerate(outs):
+        start = number * 2 * capacity
+        out[...] = filled[start : start + 2 * capacity, :].astype(bf16)
+
+
+def fetch_kernel(weights, out, sem):
+    hidden = out.shape[1]
+    there = pl.ds(pl.multiple_of(lax.axis_index("parts") * hidden, hidden), hidden)
+    copy = pltpu.make_async_copy(weights.at[0, :, there], out, sem)
+    copy.start()
+    copy.wait()
+
+
+def fetch(weights, hidden):
+    width = weights.shape[1]
+    return pl.pallas_call(
+        fetch_kernel,
+        out_shape=pltpu.VMEM((width, hidden), bf16),
+        in_specs=[hbm],
+        out_specs=vmem,
+        scratch_shapes=[pltpu.SemaphoreType.DMA],
+        cost_estimate=pl.CostEstimate(
+            flops=0, bytes_accessed=4 * width * hidden, transcendentals=0
+        ),
+        compiler_params=pltpu.CompilerParams(vmem_limit_bytes=mib),
+        name="fetch",
+    )(in_hbm(weights))
 
 
 def spread(rank2, count):
@@ -121,9 +142,9 @@
 
 def main_kernel(sizes, *refs):
     tensor_size, expert_size, size_group, capacity, devices, tile = sizes
-    (gathered, pieces, refs) = (refs[0], refs[1], refs[2:])
-    (router_hbm, out_hbm, gate_hbm, up_hbm, down_hbm, out, sent, kept, own_x, own_latent) = refs[:10]
-    (gate_mat, up_mat, down_mat, adapt, router, adapt_out, d_gate, d_up, d_rows, sems, small) = refs[10:]
+    slots, adapt, gate_mat, router_hbm, out_hbm, up_hbm, down_hbm = refs[:7]
+    out, sent, kept, own_x, own_latent = refs[7:12]
+    up_mat, down_mat, router, adapt_out, gate_pre, d_gate, d_up, d_rows, sems, small = refs[12:]
     part, expert = lax.axis_index("parts"), lax.axis_index("expert")
     width, hidden = gate_mat.shape
     rank2 = adapt.shape[0]
@@ -138,51 +159,38 @@
         there = pl.ds(pl.multiple_of(part * hidden + step * tile, tile), tile)
         for side, (source, held) in enumerate(
             (
-                (gate_hbm.at[0, :, there], gate_mat.at[:, here]),
                 (up_hbm.at[0, :, there], up_mat.at[:, here]),
                 (down_hbm.at[0, there, :], down_mat.at[here, :]),
             )
         ):
             copies.append(pltpu.make_async_copy(source, held, sems.at[side, step]))
+
+    def arrived(number):
+        copies[number].wait()
+        if number + ahead < len(copies):
+            copies[number + ahead].start()
+
     half_here = pl.ds(pl.multiple_of(part * hidden, hidden), hidden)
     minor = [
         pltpu.make_async_copy(router_hbm, router, small.at[0]),
         pltpu.make_async_copy(out_hbm.at[:, :, half_here], adapt_out, small.at[1]),
     ]
-    if len(pieces) == 1:
-        minor.append(pltpu.make_async_copy(pieces[0], adapt, small.at[2]))
-    else:
-        own = lax.axis_index("tensor")
-        cols = pieces[0].shape[1]
-        for flip, piece in enumerate(pieces):
-            first = pl.multiple_of(lax.bitwise_xor(own, flip) * cols, cols)
-            minor.append(
-                pltpu.make_async_copy(
-                    piece.at[:rank2, :], adapt.at[:, pl.ds(first, cols)], small.at[2 + flip]
-                )
-            )
     for copy in minor + copies[:ahead]:
         copy.start()
 
-    def arrived(number):
-        copies[number].wait()
-        if number + ahead < len(copies):
-            copies[number + ahead].start()
-
-    sources = gathered.shape[0]
-    slot_x = jnp.concatenate(
-        [gathered[k, :capacity, :].astype(f32) for k in range(sources)], axis=0
-    )
+    held = [ref[...].astype(f32) for ref in slots]
+    slot_x = jnp.concatenate([rows_of[:capacity] for rows_of in held], axis=0)
     x = slot_x[:, :width].astype(bf16)
-    cot = jnp.concatenate(
-        [gathered[k, capacity:, :width].astype(f32) for k in range(sources)], axis=0
-    ).astype(bf16)
+    cot = jnp.concatenate([rows_of[capacity:, :width] for rows_of in held], axis=0).astype(bf16)
     route0 = slot_x[:, width : width + 1]
     route1 = slot_x[:, width + 1 : width + 2]
     used = slot_x[:, width + 2 : width + 3]
     token = slot_x[:, width + 3 : width + 4]
     expert_f = expert.astype(f32)
-    group = lax.div(iota((rows, devices), 0), capacity) * size_group
+    slot_id = iota((rows, devices), 0)
+    source = lax.bitwise_xor(lax.div(lax.rem(slot_id, part_rows), capacity), expert)
+    slot_part = jnp.where(slot_id < part_rows, part, 1 - part)
+    group = (slot_part * expert_size + source) * size_group
     dispatch = ((iota((rows, devices), 1) - group).astype(f32) == token) & (used > 0.5)
     dispatch = jnp.where(dispatch, 1.0, 0.0).astype(bf16)
     for copy in minor:
@@ -199,20 +207,22 @@
     latent = dot(x, adapt[...], 1, 1).astype(bf16)
     latent_gate, latent_up = latent[:, :rank], latent[:, rank:]
 
+    wide = min(hidden, 1024)
+    for step in range(hidden // wide):
+        here = pl.ds(step * wide, wide)
+        gate_pre[:, here] = dot(x, gate_mat[:, here], 1, 0) + adapter_scale * dot(
+            latent_gate, adapt_out[0, :, here], 1, 0
+        )
     gate_share = jnp.zeros((rows, 1), f32)
     share_gate = jnp.zeros((rows, rank), f32)
     share_up = jnp.zeros((rows, rank), f32)
     for step in range(tiles):
         here = pl.ds(step * tile, tile)
-        gate_out = adapt_out[0, :, here]
-        up_out = adapt_out[1, :, here]
-        gate_val = adapter_scale * dot(latent_gate, gate_out, 1, 0)
-        up_val = adapter_scale * dot(latent_up, up_out, 1, 0)
-        arrived(3 * step)
-        gate_val = gate_val + dot(x, gate_mat[:, here], 1, 0)
-        arrived(3 * step + 1)
+        gate_val = gate_pre[:, here]
+        up_val = adapter_scale * dot(latent_up, adapt_out[1, :, here], 1, 0)
+        arrived(2 * step)
         up_val = up_val + dot(x, up_mat[:, here], 1, 0)
-        arrived(3 * step + 2)
+        arrived(2 * step + 1)
         returned = dot(cot, down_mat[here, :], 1, 1)
         sig = jax.nn.sigmoid(gate_val)
         activated = gate_val * sig
@@ -222,8 +232,8 @@
         d_up_tile = (d_hidden * activated).astype(bf16)
         d_gate[:, here] = d_gate_tile
         d_up[:, here] = d_up_tile
-        share_gate = share_gate + dot(d_gate_tile, gate_out, 1, 1)
-        share_up = share_up + dot(d_up_tile, up_out, 1, 1)
+        share_gate = share_gate + dot(d_gate_tile, adapt_out[0, :, here], 1, 1)
+        share_up = share_up + dot(d_up_tile, adapt_out[1, :, here], 1, 1)
         added = dot(d_gate_tile, gate_mat[:, here], 1, 1) + dot(d_up_tile, up_mat[:, here], 1, 1)
         if step == 0:
             d_rows[...] = added
@@ -243,22 +253,20 @@
     flat = jnp.where(mine, flat, 0.0).astype(bf16)
     target, source = iota((devices, rows), 0), iota((devices, rows), 1)
     to_expert = lax.rem(lax.div(target, tensor_size), expert_size) == expert
-    to_part = lax.div(target, tensor_size * expert_size) == lax.div(source, part_rows)
+    source_part = jnp.where(source < part_rows, part, 1 - part)
+    to_part = lax.div(target, tensor_size * expert_size) == source_part
     goes = jnp.where(to_expert & to_part, 1.0, 0.0).astype(bf16)
     latent_grads = dot(goes, flat, 1, 0).astype(bf16)
     half, half_lanes = width // 2, lanes // 2
     out[:, 0, :] = jnp.concatenate([token_grads[:, :half], latent_grads[:, :half_lanes]], axis=1)
     out[:, 1, :] = jnp.concatenate([token_grads[:, half:], latent_grads[:, half_lanes:]], axis=1)
 
-    def of_part(array, own):
-        top, bottom = array[:part_rows, :], array[part_rows:, :]
-        return jnp.where((part == 0) == own, top, bottom)
-
     d_gate_all, d_up_all = d_gate[...].astype(f32), d_up[...].astype(f32)
-    for ref, own in ((sent, False), (kept, True)):
-        ref[...] = jnp.concatenate([of_part(d_gate_all, own), of_part(d_up_all, own)], 0).astype(bf16)
-    own_x[...] = of_part(x.astype(f32), True).astype(bf16)
-    own_latent[...] = of_part(latent.astype(f32), True).astype(bf16)
+    for ref, first in ((kept, 0), (sent, part_rows)):
+        rows_of = slice(first, first + part_rows)
+        ref[...] = jnp.concatenate([d_gate_all[rows_of], d_up_all[rows_of]], axis=0).astype(bf16)
+    own_x[...] = slot_x[:part_rows, :width].astype(bf16)
+    own_latent[...] = latent.astype(f32)[:part_rows].astype(bf16)
 
 
 def up_kernel(kept, received, latent, out):
@@ -331,32 +339,44 @@
             for flip in range(1, tensor_size)
         ]
         group_rows = pieces
-        held = (len(pieces), bundle_rows - rank2, col_width)
     else:
         pieces = [lax.all_gather(adapt_in, "tensor", axis=1, tiled=True)]
         group_rows = [
             lax.all_gather(rows, "tensor", axis=0, tiled=True) for rows in (tokens, cotangent)
-        ]
-        held = (2, size_group, width)
-    packed = pl.pallas_call(
-        lambda *refs: pack_kernel(capacity, rank2, *refs),
-        out_shape=jax.ShapeDtypeStruct((parts * experts, 2 * capacity, width + extra), bf16),
-        in_specs=[hbm] * (1 + len(group_rows)),
-        out_specs=vmem,
+        ] + pieces
+    gate_half = fetch(w_gate, hidden)
+
+    def pack(*refs):
+        inputs, outputs = refs[: 1 + len(group_rows)], refs[2 + len(group_rows) :]
+        pack_kernel(
+            capacity, rank2, len(pieces), *inputs, outputs[:experts], *outputs[experts:]
+        )
+
+    *packed, adapt = pl.pallas_call(
+        pack,
+        out_shape=(
+            *(jax.ShapeDtypeStruct((2 * capacity, width + extra), bf16),) * experts,
+            jax.ShapeDtypeStruct((rank2, width), bf16),
+        ),
+        in_specs=[hbm] + [vmem] * (1 + len(group_rows)),
+        out_specs=[vmem] * (experts + 1),
         scratch_shapes=[
             pltpu.SMEM(routes.shape[::-1], jnp.int32),
-            pltpu.VMEM(held, bf16),
-            pltpu.SemaphoreType.DMA((1 + len(group_rows),)),
+            pltpu.SemaphoreType.DMA,
         ],
-        compiler_params=pltpu.CompilerParams(vmem_limit_bytes=32 * mib),
+        compiler_params=pltpu.CompilerParams(vmem_limit_bytes=16 * mib),
         name="pack",
-    )(in_hbm(routes.T), *[in_hbm(piece) for piece in group_rows])
-    gathered = lax.all_to_all(packed, ("parts", "expert"), split_axis=0, concat_axis=0, tiled=True)
-
+    )(in_hbm(routes.T), *group_rows, pltpu.with_memory_space_constraint(gate_half, pltpu.VMEM))
+    plane = range(parts * experts)
+    slots = [packed[0]] + [
+        lax.ppermute(packed[flip % experts], ("parts", "expert"), [(i, i ^ flip) for i in plane])
+        for flip in plane
+        if flip > 0
+    ]
     sizes = (tensor_size, expert_size, size_group, capacity, devices, tile)
 
     def main(*refs):
-        main_kernel(sizes, refs[0], refs[1 : 1 + len(pieces)], *refs[1 + len(pieces) :])
+        main_kernel(sizes, refs[: len(slots)], *refs[len(slots) :])
 
     out, sent, kept, own_x, own_latent = pl.pallas_call(
         main,
@@ -367,34 +387,33 @@
             jax.ShapeDtypeStruct((part_rows, width), bf16),
             jax.ShapeDtypeStruct((part_rows, rank2), bf16),
         ),
-        in_specs=[vmem] + [hbm] * (len(pieces) + 5),
+        in_specs=[vmem] * (len(slots) + 2) + [hbm] * 4,
         out_specs=[vmem] * 5,
         scratch_shapes=[
             pltpu.VMEM((width, hidden), bf16),
-            pltpu.VMEM((width, hidden), bf16),
             pltpu.VMEM((hidden, width), bf16),
-            pltpu.VMEM((rank2, width), bf16),
             pltpu.VMEM((experts, width), bf16),
             pltpu.VMEM((2, rank2 // 2, hidden), bf16),
+            pltpu.VMEM((rows, hidden), f32),
             pltpu.VMEM((rows, hidden), bf16),
             pltpu.VMEM((rows, hidden), bf16),
             pltpu.VMEM((rows, width), f32),
-            pltpu.SemaphoreType.DMA((3, tiles)),
-            pltpu.SemaphoreType.DMA((2 + len(pieces),)),
+            pltpu.SemaphoreType.DMA((2, tiles)),
+            pltpu.SemaphoreType.DMA((2,)),
         ],
         cost_estimate=pl.CostEstimate(
             flops=10 * rows * width * hidden,
-            bytes_accessed=6 * width * hidden,
+            bytes_accessed=2 * width * hidden,
             transcendentals=rows * hidden,
         ),
-        compiler_params=pltpu.CompilerParams(vmem_limit_bytes=50 * mib),
+        compiler_params=pltpu.CompilerParams(vmem_limit_bytes=38 * mib),
         name="main",
     )(
-        gathered,
-        *[in_hbm(piece) for piece in pieces],
+        *slots,
+        adapt,
+        pltpu.with_memory_space_constraint(gate_half, pltpu.VMEM),
         in_hbm(router.T),
         in_hbm(adapter_up[0]),
-        in_hbm(w_gate),
         in_hbm(w_up),
         in_hbm(w_down),
     )

time: 58.7 us -> 55.5 us (0.945)
  blocking collectives: 9.84 us -> 0 us
  starting transfers between devices: 10.7 us -> 18.9 us
  waiting for transfers between devices: 12.2 us -> 10.1 us
  Pallas kernels: 24.3 us -> 25.6 us
  local copies, waits for them, and re-layouts: 0.65 us -> 0 us
    all_to_all x1 -> x0, blocking collectives: 9.84 us -> none  [per_device(): lax.all_to_all(packed, ('parts', 'expert'), split_axis=0, concat_axis=0,...]
    ppermute x0 -> x7, starting transfers between devices: none -> 6.88 us  [per_device(): lax.ppermute(packed[flip % experts], ('parts', 'expert'), [(i, i ^ flip)...]
    ppermute x3, waiting for transfers between devices: 5.57 us -> 0.98 us  [per_device(): lax.ppermute(bundle, 'tensor', [(i, i ^ flip) for i in range(tensor_size)])]
    pallas_call x1 -> x2, Pallas kernels: 1.16 us -> 5.6 us  [the longest x1 4.58 us: fetch(): pl.pallas_call(fetch_kernel, out_shape=pltpu.VMEM((width, hidden), bf16),...]
    pallas_call x1, Pallas kernels: 20.1 us -> 17 us  [per_device(): pl.pallas_call(main, out_shape=(jax.ShapeDtypeStruct((devices, 2, (width...]
    ppermute x0 -> x7, waiting for transfers between devices: none -> 2.47 us  [per_device(): lax.ppermute(packed[flip % experts], ('parts', 'expert'), [(i, i ^ flip)...]
    all_to_all x1, starting transfers between devices: 3.09 us -> 4.38 us  [per_device(): lax.all_to_all(out, every_axis, split_axis=0, concat_axis=0, tiled=True)]
    unnamed x8 -> x0, local copies, waits for them, and re-layouts: 0.65 us -> none
  transfers between devices with their start and end apart: 5 -> 12, of which waited for: 4 -> 6; matrix products, arithmetic and copies ran while one was open for 0% -> 0% of each run, Pallas kernels for 2% -> 10%
where the time goes in v2:
time: 55.5 us; the launch traced here: 55.2 us
  Pallas kernels  25.6 us (46%)
  starting transfers between devices  18.9 us (34%)
  waiting for transfers between devices  10.1 us (18%)
  between operations  0.69 us (1%)
    pallas_call x1, Pallas kernels, per_device(): pl.pallas_call(main, out_shape=(jax.ShapeDtypeStruct((devices, 2, (width...  17 us
    ppermute x7, starting transfers between devices, per_device(): lax.ppermute(packed[flip % experts], ('parts', 'expert'), [(i, i ^ flip)...  6.88 us
    ppermute x3, starting transfers between devices, per_device(): lax.ppermute(bundle, 'tensor', [(i, i ^ flip) for i in range(tensor_size)])  5.76 us
    pallas_call x1, Pallas kernels, fetch(): pl.pallas_call(fetch_kernel, out_shape=pltpu.VMEM((width, hidden), bf16),...  4.58 us
    all_to_all x1, starting transfers between devices, per_device(): lax.all_to_all(out, every_axis, split_axis=0, concat_axis=0, tiled=True)  4.38 us
    ppermute x1, waiting for transfers between devices, per_device(): other = lax.ppermute(sent, 'parts', [(0, 1), (1, 0)])  3.61 us
    all_to_all x1, waiting for transfers between devices, per_device(): lax.all_to_all(out, every_axis, split_axis=0, concat_axis=0, tiled=True)  3.02 us
    ppermute x7, waiting for transfers between devices, per_device(): lax.ppermute(packed[flip % experts], ('parts', 'expert'), [(i, i ^ flip)...  2.47 us
  transfers between devices with their start and end apart: 12, of which 6 were waited for; matrix products, arithmetic and copies ran while one was open for 0% of the time, Pallas kernels for 10%

profile of v2, /device:TPU:0, one launch (start us, length us, event | category | flops | bytes accessed | tf_op | source)
XLA Modules:
  0.0 55.2 jit_solution(7192772672430842239)
XLA Ops:
  0.6 0.9 %bundle.1.refs_1_ = bf16[48,768]{1,0:T(8,128)(2,1)S(1)} custom-call(bf16[1,3072]{1,0:T(2,128)(2,1)} %tokens_hbm.1, bf16[1,3072]{1,0:T(2,128)(2,1)} %cotangent_hbm.1, bf16[32,768]{1,0:T(8,128)(2,1)} %bitcast.12), custom_call_target="tpu_custom_call" | custom-call | tf_op jit(solution)/shard_map/bundle/pallas_call | solution.py:328
  1.5 5.1 %collective-permute-start.2 = (bf16[48,768]{1,0:T(8,128)(2,1)S(1)}, bf16[48,768]{1,0:T(8,128)(2,1)S(1)}, u32[]{:S(2)}, u32[]{:S(2)}) collective-permute-start(bf16[48,768]{1,0:T(8,128)(2,1)S(1)} %bundle.1.refs_1_), channel_id=1, source_target_pairs={{0,3},{1,2},{2,1},{3,0},{4,7},{5,6},{6,5},{7,4},{8,11},{9,10},{10,... | collective-permute-start | bytes 221192 | tf_op jit(solution)/shard_map/ppermute | solution.py:338
  6.6 0.0 collective-permute-start.1
  6.6 0.6 %collective-permute-start = (bf16[48,768]{1,0:T(8,128)(2,1)S(1)}, bf16[48,768]{1,0:T(8,128)(2,1)S(1)}, u32[]{:S(2)}, u32[]{:S(2)}) collective-permute-start(bf16[48,768]{1,0:T(8,128)(2,1)S(1)} %bundle.1.refs_1_), channel_id=1, source_target_pairs={{0,1},{1,0},{2,3},{3,2},{4,5},{5,4},{6,7},{7,6},{8,9},{9,8},{10,11... | collective-permute-start | bytes 221192 | tf_op jit(solution)/shard_map/ppermute | solution.py:338
  7.3 4.6 %fetch.1.refs_5_.refs_9_ = bf16[3072,2048]{1,0:T(8,128)(2,1)S(1)} custom-call(bf16[1,3072,4096]{2,1,0:T(8,128)(2,1)} %weights.1), custom_call_target="tpu_custom_call" | custom-call | bytes 25165824 | tf_op jit(solution)/shard_map/fetch/pallas_call | solution.py:124
  11.9 1.0 %collective-permute-done.1.refs_3_ = bf16[48,768]{1,0:T(8,128)(2,1)S(1)} collective-permute-done((bf16[48,768]{1,0:T(8,128)(2,1)S(1)}, bf16[48,768]{1,0:T(8,128)(2,1)S(1)}, u32[]{:S(2)}, u32[]{:S(2)}) %collective-permute-start.1) | collective-permute-done | bytes 73760 | tf_op jit(solution)/shard_map/ppermute | solution.py:338
  12.8 0.0 collective-permute-done.refs_2_
  12.9 1.0 %pack.1 = (bf16[4,3200]{1,0:T(4,128)(2,1)S(1)}, bf16[4,3200]{1,0:T(4,128)(2,1)S(1)}, bf16[4,3200]{1,0:T(4,128)(2,1)S(1)}, bf16[4,3200]{1,0:T(4,128)(2,1)S(1)}, bf16[32,3072]{1,0:T(8,128)(2,1)S(1)}) custom-call(s32[2,4]{1,0:T(2,128)} %bitcast.14, bf16[48,768]{1,0:T(8,128)(2,1)S(1)} %bundle.1.refs_1_, bf16[48,768]{1,0:T(8,128)(2,1)S(1)} %collective-permute-done.refs_2_, ...), custom_call_target="tpu_custom_call" | custom-call | tf_op jit(solution)/shard_map/pack/pallas_call | solution.py:355
  13.9 1.6 %collective-permute-start.6 = (bf16[4,3200]{1,0:T(4,128)(2,1)S(1)}, bf16[4,3200]{1,0:T(4,128)(2,1)S(1)}, u32[]{:S(2)}, u32[]{:S(2)}) collective-permute-start(bf16[4,3200]{1,0:T(4,128)(2,1)S(1)} %get-tuple-element.15.refs_0_), channel_id=1, source_target_pairs={{0,16},{4,20},{8,24},{12,28},{16,0},{20,4},{24,8},{28,12},{1,17},{... | collective-permute-start | bytes 76808 | tf_op jit(solution)/shard_map/ppermute | solution.py:372
  15.5 0.6 %collective-permute-start.3 = (bf16[4,3200]{1,0:T(4,128)(2,1)S(1)}, bf16[4,3200]{1,0:T(4,128)(2,1)S(1)}, u32[]{:S(2)}, u32[]{:S(2)}) collective-permute-start(bf16[4,3200]{1,0:T(4,128)(2,1)S(1)} %get-tuple-element.16), channel_id=1, source_target_pairs={{0,4},{4,0},{8,12},{12,8},{16,20},{20,16},{24,28},{28,24},{1,5},{5... | collective-permute-start | bytes 76808 | tf_op jit(solution)/shard_map/ppermute | solution.py:372
  16.1 2.4 %collective-permute-start.8 = (bf16[4,3200]{1,0:T(4,128)(2,1)S(1)}, bf16[4,3200]{1,0:T(4,128)(2,1)S(1)}, u32[]{:S(2)}, u32[]{:S(2)}) collective-permute-start(bf16[4,3200]{1,0:T(4,128)(2,1)S(1)} %get-tuple-element.17), channel_id=1, source_target_pairs={{0,24},{4,28},{8,16},{12,20},{16,8},{20,12},{24,0},{28,4},{1,25},{... | collective-permute-start | bytes 76808 | tf_op jit(solution)/shard_map/ppermute | solution.py:372
  18.5 0.5 collective-permute-start.4
  19.1 0.5 collective-permute-start.9
  19.5 1.2 %collective-permute-start.5 = (bf16[4,3200]{1,0:T(4,128)(2,1)S(1)}, bf16[4,3200]{1,0:T(4,128)(2,1)S(1)}, u32[]{:S(2)}, u32[]{:S(2)}) collective-permute-start(bf16[4,3200]{1,0:T(4,128)(2,1)S(1)} %get-tuple-element.18), channel_id=1, source_target_pairs={{0,12},{4,8},{8,4},{12,0},{16,28},{20,24},{24,20},{28,16},{1,13},{... | collective-permute-start | bytes 76808 | tf_op jit(solution)/shard_map/ppermute | solution.py:372
  20.8 0.1 collective-permute-done.8.refs_6_
  20.8 1.7 %collective-permute-done.4.refs_2_ = bf16[4,3200]{1,0:T(4,128)(2,1)S(1)} collective-permute-done((bf16[4,3200]{1,0:T(4,128)(2,1)S(1)}, bf16[4,3200]{1,0:T(4,128)(2,1)S(1)}, u32[]{:S(2)}, u32[]{:S(2)}) %collective-permute-start.4) | collective-permute-done | bytes 25632 | tf_op jit(solution)/shard_map/ppermute | solution.py:372
  22.6 0.7 %collective-permute-done.9.refs_7_ = bf16[4,3200]{1,0:T(4,128)(2,1)S(1)} collective-permute-done((bf16[4,3200]{1,0:T(4,128)(2,1)S(1)}, bf16[4,3200]{1,0:T(4,128)(2,1)S(1)}, u32[]{:S(2)}, u32[]{:S(2)}) %collective-permute-start.9) | collective-permute-done | bytes 25632 | tf_op jit(solution)/shard_map/ppermute | solution.py:372
  23.2 17.0 %main.1 = (bf16[32,2,1664]{2,1,0:T(2,128)(2,1)}, bf16[16,2048]{1,0:T(8,128)(2,1)S(1)}, bf16[16,2048]{1,0:T(8,128)(2,1)S(1)}, bf16[8,3072]{1,0:T(8,128)(2,1)S(1)}, bf16[8,32]{1,0:T(8,128)(2,1)S(1)}) custom-call(bf16[4,3200]{1,0:T(4,128)(2,1)S(1)} %get-tuple-element.15.refs_0_, bf16[4,3200]{1,0:T(4,128)(2,1)S(1)} %collective-permute-done.3.refs_1_, ...), custom_call_target="tpu_custom_call" | custom-call | flops 1006632960 | bytes 12582912 | tf_op jit(solution)/shard_map/main/pallas_call | solution.py:381
  40.2 4.4 %all-to-all-start = ((bf16[32,2,1664]{2,1,0:T(2,128)(2,1)}), bf16[32,2,1664]{2,1,0:T(2,128)(2,1)S(1)}, u32[]{:S(2)}, u32[]{:S(2)}) async-start(bf16[32,2,1664]{2,1,0:T(2,128)(2,1)} %get-tuple-element.20), calls=%async_computation | async-start | bytes 425984 | tf_op jit(solution)/shard_map/all_to_all | solution.py:421
  44.6 1.8 %collective-permute-start.10 = (bf16[16,2048]{1,0:T(8,128)(2,1)S(1)}, bf16[16,2048]{1,0:T(8,128)(2,1)S(1)}, u32[]{:S(2)}, u32[]{:S(2)}) collective-permute-start(bf16[16,2048]{1,0:T(8,128)(2,1)S(1)} %get-tuple-element.25), channel_id=1, source_target_pairs={{0,16},{16,0},{1,17},{17,1},{2,18},{18,2},{3,19},{19,3},{4,20},{20... | collective-permute-start | bytes 196616 | tf_op jit(solution)/shard_map/ppermute | solution.py:422
  46.4 3.6 %collective-permute-done.10.received = bf16[16,2048]{1,0:T(8,128)(2,1)S(1)} collective-permute-done((bf16[16,2048]{1,0:T(8,128)(2,1)S(1)}, bf16[16,2048]{1,0:T(8,128)(2,1)S(1)}, u32[]{:S(2)}, u32[]{:S(2)}) %collective-permute-start.10) | collective-permute-done | bytes 65568 | tf_op jit(solution)/shard_map/ppermute | solution.py:422
  50.0 1.1 %grad_up.1 = f32[2,16,4096]{2,1,0:T(8,128)} custom-call(bf16[16,2048]{1,0:T(8,128)(2,1)S(1)} %get-tuple-element.24.kept, bf16[16,2048]{1,0:T(8,128)(2,1)S(1)} %collective-permute-done.10.received, bf16[8,32]{1,0:T(8,128)(2,1)S(1)} %get-tuple-element.26.latent), custom_call_target="tpu_custom_call" | custom-call | flops 4194304 | bytes 524288 | tf_op jit(solution)/shard_map/grad_up/pallas_call | solution.py:423
  51.1 3.0 %all-to-all-done.received = bf16[32,2,1664]{2,1,0:T(2,128)(2,1)S(1)} async-done(((bf16[32,2,1664]{2,1,0:T(2,128)(2,1)}), bf16[32,2,1664]{2,1,0:T(2,128)(2,1)S(1)}, u32[]{:S(2)}, u32[]{:S(2)}) %all-to-all-start) | async-done | bytes 213024 | tf_op jit(solution)/shard_map/all_to_all | solution.py:421
  54.1 1.0 %last.1 = (bf16[1,3072]{1,0:T(2,128)(2,1)}, f32[32,768]{1,0:T(8,128)}) custom-call(bf16[32,2,1664]{2,1,0:T(2,128)(2,1)S(1)} %all-to-all-done.received, bf16[8,3072]{1,0:T(8,128)(2,1)S(1)} %get-tuple-element.21.x_cols), custom_call_target="tpu_custom_call" | custom-call | tf_op jit(solution)/shard_map/last/pallas_call | solution.py:443
  (6 shorter events, 0.0 us)
Async XLA Ops:
  1.5 10.4 %collective-permute-start.2 = (bf16[48,768]{1,0:T(8,128)(2,1)S(1)}, bf16[48,768]{1,0:T(8,128)(2,1)S(1)}, u32[]{:S(2)}, u32[]{:S(2)}) collective-permute-start(bf16[48,768]{1,0:T(8,128)(2,1)S(1)} %bundle.1.refs_1_), channel_id=1, source_target_pairs={{0,3},{1,2},{2,1},{3,0},{4,7},{5,6},{6,5},{7,4},{8,11},{9,10},{10,... | collective-permute-start | bytes 221192 | tf_op jit(solution)/shard_map/ppermute | solution.py:338
  6.6 6.2 %collective-permute-start.1 = (bf16[48,768]{1,0:T(8,128)(2,1)S(1)}, bf16[48,768]{1,0:T(8,128)(2,1)S(1)}, u32[]{:S(2)}, u32[]{:S(2)}) collective-permute-start(bf16[48,768]{1,0:T(8,128)(2,1)S(1)} %bundle.1.refs_1_), channel_id=1, source_target_pairs={{0,2},{1,3},{2,0},{3,1},{4,6},{5,7},{6,4},{7,5},{8,10},{9,11},{10,... | collective-permute-start | bytes 221192 | tf_op jit(solution)/shard_map/ppermute | solution.py:338
  6.6 6.2 %collective-permute-start = (bf16[48,768]{1,0:T(8,128)(2,1)S(1)}, bf16[48,768]{1,0:T(8,128)(2,1)S(1)}, u32[]{:S(2)}, u32[]{:S(2)}) collective-permute-start(bf16[48,768]{1,0:T(8,128)(2,1)S(1)} %bundle.1.refs_1_), channel_id=1, source_target_pairs={{0,1},{1,0},{2,3},{3,2},{4,5},{5,4},{6,7},{7,6},{8,9},{9,8},{10,11... | collective-permute-start | bytes 221192 | tf_op jit(solution)/shard_map/ppermute | solution.py:338
  13.9 5.2 %collective-permute-start.6 = (bf16[4,3200]{1,0:T(4,128)(2,1)S(1)}, bf16[4,3200]{1,0:T(4,128)(2,1)S(1)}, u32[]{:S(2)}, u32[]{:S(2)}) collective-permute-start(bf16[4,3200]{1,0:T(4,128)(2,1)S(1)} %get-tuple-element.15.refs_0_), channel_id=1, source_target_pairs={{0,16},{4,20},{8,24},{12,28},{16,0},{20,4},{24,8},{28,12},{1,17},{... | collective-permute-start | bytes 76808 | tf_op jit(solution)/shard_map/ppermute | solution.py:372
  15.5 4.1 %collective-permute-start.7 = (bf16[4,3200]{1,0:T(4,128)(2,1)S(1)}, bf16[4,3200]{1,0:T(4,128)(2,1)S(1)}, u32[]{:S(2)}, u32[]{:S(2)}) collective-permute-start(bf16[4,3200]{1,0:T(4,128)(2,1)S(1)} %get-tuple-element.16), channel_id=1, source_target_pairs={{0,20},{4,16},{8,28},{12,24},{16,4},{20,0},{24,12},{28,8},{1,21},{... | collective-permute-start | bytes 76808 | tf_op jit(solution)/shard_map/ppermute | solution.py:372
  15.5 5.3 %collective-permute-start.3 = (bf16[4,3200]{1,0:T(4,128)(2,1)S(1)}, bf16[4,3200]{1,0:T(4,128)(2,1)S(1)}, u32[]{:S(2)}, u32[]{:S(2)}) collective-permute-start(bf16[4,3200]{1,0:T(4,128)(2,1)S(1)} %get-tuple-element.16), channel_id=1, source_target_pairs={{0,4},{4,0},{8,12},{12,8},{16,20},{20,16},{24,28},{28,24},{1,5},{5... | collective-permute-start | bytes 76808 | tf_op jit(solution)/shard_map/ppermute | solution.py:372
  16.1 4.8 %collective-permute-start.8 = (bf16[4,3200]{1,0:T(4,128)(2,1)S(1)}, bf16[4,3200]{1,0:T(4,128)(2,1)S(1)}, u32[]{:S(2)}, u32[]{:S(2)}) collective-permute-start(bf16[4,3200]{1,0:T(4,128)(2,1)S(1)} %get-tuple-element.17), channel_id=1, source_target_pairs={{0,24},{4,28},{8,16},{12,20},{16,8},{20,12},{24,0},{28,4},{1,25},{... | collective-permute-start | bytes 76808 | tf_op jit(solution)/shard_map/ppermute | solution.py:372
  18.5 4.0 %collective-permute-start.4 = (bf16[4,3200]{1,0:T(4,128)(2,1)S(1)}, bf16[4,3200]{1,0:T(4,128)(2,1)S(1)}, u32[]{:S(2)}, u32[]{:S(2)}) collective-permute-start(bf16[4,3200]{1,0:T(4,128)(2,1)S(1)} %get-tuple-element.17), channel_id=1, source_target_pairs={{0,8},{4,12},{8,0},{12,4},{16,24},{20,28},{24,16},{28,20},{1,9},{5... | collective-permute-start | bytes 76808 | tf_op jit(solution)/shard_map/ppermute | solution.py:372
  19.1 4.2 %collective-permute-start.9 = (bf16[4,3200]{1,0:T(4,128)(2,1)S(1)}, bf16[4,3200]{1,0:T(4,128)(2,1)S(1)}, u32[]{:S(2)}, u32[]{:S(2)}) collective-permute-start(bf16[4,3200]{1,0:T(4,128)(2,1)S(1)} %get-tuple-element.18), channel_id=1, source_target_pairs={{0,28},{4,24},{8,20},{12,16},{16,12},{20,8},{24,4},{28,0},{1,29},{... | collective-permute-start | bytes 76808 | tf_op jit(solution)/shard_map/ppermute | solution.py:372
  19.5 3.7 %collective-permute-start.5 = (bf16[4,3200]{1,0:T(4,128)(2,1)S(1)}, bf16[4,3200]{1,0:T(4,128)(2,1)S(1)}, u32[]{:S(2)}, u32[]{:S(2)}) collective-permute-start(bf16[4,3200]{1,0:T(4,128)(2,1)S(1)} %get-tuple-element.18), channel_id=1, source_target_pairs={{0,12},{4,8},{8,4},{12,0},{16,28},{20,24},{24,20},{28,16},{1,13},{... | collective-permute-start | bytes 76808 | tf_op jit(solution)/shard_map/ppermute | solution.py:372
  40.2 14.0 %all-to-all-start = ((bf16[32,2,1664]{2,1,0:T(2,128)(2,1)}), bf16[32,2,1664]{2,1,0:T(2,128)(2,1)S(1)}, u32[]{:S(2)}, u32[]{:S(2)}) async-start(bf16[32,2,1664]{2,1,0:T(2,128)(2,1)} %get-tuple-element.20), calls=%async_computation | async-start | bytes 425984 | tf_op jit(solution)/shard_map/all_to_all | solution.py:421
  44.6 5.4 %collective-permute-start.10 = (bf16[16,2048]{1,0:T(8,128)(2,1)S(1)}, bf16[16,2048]{1,0:T(8,128)(2,1)S(1)}, u32[]{:S(2)}, u32[]{:S(2)}) collective-permute-start(bf16[16,2048]{1,0:T(8,128)(2,1)S(1)} %get-tuple-element.25), channel_id=1, source_target_pairs={{0,16},{16,0},{1,17},{17,1},{2,18},{18,2},{3,19},{19,3},{4,20},{20... | collective-permute-start | bytes 196616 | tf_op jit(solution)/shard_map/ppermute | solution.py:422

commit v3 on v2

--- a/solution.py
+++ b/solution.py
@@ -111,28 +111,38 @@
         out[...] = filled[start : start + 2 * capacity, :].astype(bf16)
 
 
-def fetch_kernel(weights, out, sem):
+def fetch_kernel(weights, router, adapt_out, out, router_to, adapt_out_to, sems):
     hidden = out.shape[1]
     there = pl.ds(pl.multiple_of(lax.axis_index("parts") * hidden, hidden), hidden)
-    copy = pltpu.make_async_copy(weights.at[0, :, there], out, sem)
-    copy.start()
-    copy.wait()
-
-
-def fetch(weights, hidden):
+    copies = [
+        pltpu.make_async_copy(weights.at[0, :, there], out, sems.at[0]),
+        pltpu.make_async_copy(router, router_to, sems.at[1]),
+        pltpu.make_async_copy(adapt_out.at[:, :, there], adapt_out_to, sems.at[2]),
+    ]
+    for copy in copies:
+        copy.start()
+    for copy in copies:
+        copy.wait()
+
+
+def fetch(weights, router, adapt_out, hidden):
     width = weights.shape[1]
     return pl.pallas_call(
         fetch_kernel,
-        out_shape=pltpu.VMEM((width, hidden), bf16),
-        in_specs=[hbm],
-        out_specs=vmem,
-        scratch_shapes=[pltpu.SemaphoreType.DMA],
+        out_shape=(
+            pltpu.VMEM((width, hidden), bf16),
+            pltpu.VMEM(router.shape, bf16),
+            pltpu.VMEM((*adapt_out.shape[:2], hidden), bf16),
+        ),
+        in_specs=[hbm] * 3,
+        out_specs=[vmem] * 3,
+        scratch_shapes=[pltpu.SemaphoreType.DMA((3,))],
         cost_estimate=pl.CostEstimate(
             flops=0, bytes_accessed=4 * width * hidden, transcendentals=0
         ),
         compiler_params=pltpu.CompilerParams(vmem_limit_bytes=mib),
         name="fetch",
-    )(in_hbm(weights))
+    )(in_hbm(weights), in_hbm(router), in_hbm(adapt_out))
 
 
 def spread(rank2, count):
@@ -142,9 +152,9 @@
 
 def main_kernel(sizes, *refs):
     tensor_size, expert_size, size_group, capacity, devices, tile = sizes
-    slots, adapt, gate_mat, router_hbm, out_hbm, up_hbm, down_hbm = refs[:7]
+    slots, adapt, gate_mat, router, adapt_out, up_hbm, down_hbm = refs[:7]
     out, sent, kept, own_x, own_latent = refs[7:12]
-    up_mat, down_mat, router, adapt_out, gate_pre, d_gate, d_up, d_rows, sems, small = refs[12:]
+    up_mat, down_mat, gate_pre, d_gate, d_up, d_rows, sems = refs[12:]
     part, expert = lax.axis_index("parts"), lax.axis_index("expert")
     width, hidden = gate_mat.shape
     rank2 = adapt.shape[0]
@@ -170,12 +180,7 @@
         if number + ahead < len(copies):
             copies[number + ahead].start()
 
-    half_here = pl.ds(pl.multiple_of(part * hidden, hidden), hidden)
-    minor = [
-        pltpu.make_async_copy(router_hbm, router, small.at[0]),
-        pltpu.make_async_copy(out_hbm.at[:, :, half_here], adapt_out, small.at[1]),
-    ]
-    for copy in minor + copies[:ahead]:
+    for copy in copies[:ahead]:
         copy.start()
 
     held = [ref[...].astype(f32) for ref in slots]
@@ -193,9 +198,6 @@
     group = (slot_part * expert_size + source) * size_group
     dispatch = ((iota((rows, devices), 1) - group).astype(f32) == token) & (used > 0.5)
     dispatch = jnp.where(dispatch, 1.0, 0.0).astype(bf16)
-    for copy in minor:
-        copy.wait()
-
     logits = dot(x, router[...], 1, 1)
     ids = iota(logits.shape, 1).astype(f32)
     signs = jnp.where(ids == route0, 1.0, 0.0) - jnp.where(ids == route1, 1.0, 0.0)
@@ -344,7 +346,7 @@
         group_rows = [
             lax.all_gather(rows, "tensor", axis=0, tiled=True) for rows in (tokens, cotangent)
         ] + pieces
-    gate_half = fetch(w_gate, hidden)
+    gate_half, router_near, adapt_out_near = fetch(w_gate, router.T, adapter_up[0], hidden)
 
     def pack(*refs):
         inputs, outputs = refs[: 1 + len(group_rows)], refs[2 + len(group_rows) :]
@@ -387,19 +389,16 @@
             jax.ShapeDtypeStruct((part_rows, width), bf16),
             jax.ShapeDtypeStruct((part_rows, rank2), bf16),
         ),
-        in_specs=[vmem] * (len(slots) + 2) + [hbm] * 4,
+        in_specs=[vmem] * (len(slots) + 4) + [hbm] * 2,
         out_specs=[vmem] * 5,
         scratch_shapes=[
             pltpu.VMEM((width, hidden), bf16),
             pltpu.VMEM((hidden, width), bf16),
-            pltpu.VMEM((experts, width), bf16),
-            pltpu.VMEM((2, rank2 // 2, hidden), bf16),
             pltpu.VMEM((rows, hidden), f32),
             pltpu.VMEM((rows, hidden), bf16),
             pltpu.VMEM((rows, hidden), bf16),
             pltpu.VMEM((rows, width), f32),
             pltpu.SemaphoreType.DMA((2, tiles)),
-            pltpu.SemaphoreType.DMA((2,)),
         ],
         cost_estimate=pl.CostEstimate(
             flops=10 * rows * width * hidden,
@@ -412,8 +411,10 @@
         *slots,
         adapt,
         pltpu.with_memory_space_constraint(gate_half, pltpu.VMEM),
-        in_hbm(router.T),
-        in_hbm(adapter_up[0]),
+        *[
+            pltpu.with_memory_space_constraint(near, pltpu.VMEM)
+            for near in (router_near, adapt_out_near)
+        ],
         in_hbm(w_up),
         in_hbm(w_down),
     )

time: 55.5 us -> 56.7 us (1.022)
  Pallas kernels: 25.6 us -> 26.8 us
    pallas_call x1, Pallas kernels: 17 us -> 18.2 us  [per_device(): pl.pallas_call(main, out_shape=(jax.ShapeDtypeStruct((devices, 2, (width...]
where the time goes in v3:
time: 56.7 us; the launch traced here: 56.4 us
  Pallas kernels  26.8 us (47%)
  starting transfers between devices  18.9 us (33%)
  waiting for transfers between devices  10.1 us (18%)
  between operations  0.69 us (1%)
    pallas_call x1, Pallas kernels, per_device(): pl.pallas_call(main, out_shape=(jax.ShapeDtypeStruct((devices, 2, (width...  18.2 us
    ppermute x7, starting transfers between devices, per_device(): lax.ppermute(packed[flip % experts], ('parts', 'expert'), [(i, i ^ flip)...  6.88 us
    ppermute x3, starting transfers between devices, per_device(): lax.ppermute(bundle, 'tensor', [(i, i ^ flip) for i in range(tensor_size)])  5.76 us
    pallas_call x1, Pallas kernels, fetch(): pl.pallas_call(fetch_kernel, out_shape=(pltpu.VMEM((width, hidden), bf16)...  4.6 us
    all_to_all x1, starting transfers between devices, per_device(): lax.all_to_all(out, every_axis, split_axis=0, concat_axis=0, tiled=True)  4.4 us
    ppermute x1, waiting for transfers between devices, per_device(): other = lax.ppermute(sent, 'parts', [(0, 1), (1, 0)])  3.61 us
    all_to_all x1, waiting for transfers between devices, per_device(): lax.all_to_all(out, every_axis, split_axis=0, concat_axis=0, tiled=True)  3.02 us
    ppermute x7, waiting for transfers between devices, per_device(): lax.ppermute(packed[flip % experts], ('parts', 'expert'), [(i, i ^ flip)...  2.47 us
  transfers between devices with their start and end apart: 12, of which 6 were waited for; matrix products, arithmetic and copies ran while one was open for 0% of the time, Pallas kernels for 10%

profile of v3, /device:TPU:0, one launch (start us, length us, event | category | flops | bytes accessed | tf_op | source)
XLA Modules:
  0.0 56.4 jit_solution(1138587961984174256)
XLA Ops:
  0.6 0.9 %bundle.1.refs_1_ = bf16[48,768]{1,0:T(8,128)(2,1)S(1)} custom-call(bf16[1,3072]{1,0:T(2,128)(2,1)} %tokens_hbm.1, bf16[1,3072]{1,0:T(2,128)(2,1)} %cotangent_hbm.1, bf16[32,768]{1,0:T(8,128)(2,1)} %bitcast.12), custom_call_target="tpu_custom_call" | custom-call | tf_op jit(solution)/shard_map/bundle/pallas_call | solution.py:330
  1.5 5.1 %collective-permute-start.2 = (bf16[48,768]{1,0:T(8,128)(2,1)S(1)}, bf16[48,768]{1,0:T(8,128)(2,1)S(1)}, u32[]{:S(2)}, u32[]{:S(2)}) collective-permute-start(bf16[48,768]{1,0:T(8,128)(2,1)S(1)} %bundle.1.refs_1_), channel_id=1, source_target_pairs={{0,3},{1,2},{2,1},{3,0},{4,7},{5,6},{6,5},{7,4},{8,11},{9,10},{10,... | collective-permute-start | bytes 221192 | tf_op jit(solution)/shard_map/ppermute | solution.py:340
  6.6 0.0 collective-permute-start.1
  6.6 0.6 %collective-permute-start = (bf16[48,768]{1,0:T(8,128)(2,1)S(1)}, bf16[48,768]{1,0:T(8,128)(2,1)S(1)}, u32[]{:S(2)}, u32[]{:S(2)}) collective-permute-start(bf16[48,768]{1,0:T(8,128)(2,1)S(1)} %bundle.1.refs_1_), channel_id=1, source_target_pairs={{0,1},{1,0},{2,3},{3,2},{4,5},{5,4},{6,7},{7,6},{8,9},{9,8},{10,11... | collective-permute-start | bytes 221192 | tf_op jit(solution)/shard_map/ppermute | solution.py:340
  7.3 4.6 %fetch.1 = (bf16[3072,2048]{1,0:T(8,128)(2,1)S(1)}, bf16[4,3072]{1,0:T(4,128)(2,1)S(1)}, bf16[2,16,2048]{2,1,0:T(8,128)(2,1)S(1)}) custom-call(bf16[1,3072,4096]{2,1,0:T(8,128)(2,1)} %weights.1, bf16[4,3072]{1,0:T(4,128)(2,1)} %bitcast.13, bf16[2,16,4096]{2,1,0:T(8,128)(2,1)} %bitcast.11), custom_call_target="tpu_custom_call" | custom-call | bytes 25165824 | tf_op jit(solution)/shard_map/fetch/pallas_call | solution.py:130
  11.9 0.0 collective-permute-done.2.refs_4_
  11.9 1.0 %collective-permute-done.1.refs_3_ = bf16[48,768]{1,0:T(8,128)(2,1)S(1)} collective-permute-done((bf16[48,768]{1,0:T(8,128)(2,1)S(1)}, bf16[48,768]{1,0:T(8,128)(2,1)S(1)}, u32[]{:S(2)}, u32[]{:S(2)}) %collective-permute-start.1) | collective-permute-done | bytes 73760 | tf_op jit(solution)/shard_map/ppermute | solution.py:340
  12.9 1.0 %pack.1 = (bf16[4,3200]{1,0:T(4,128)(2,1)S(1)}, bf16[4,3200]{1,0:T(4,128)(2,1)S(1)}, bf16[4,3200]{1,0:T(4,128)(2,1)S(1)}, bf16[4,3200]{1,0:T(4,128)(2,1)S(1)}, bf16[32,3072]{1,0:T(8,128)(2,1)S(1)}) custom-call(s32[2,4]{1,0:T(2,128)} %bitcast.14, bf16[48,768]{1,0:T(8,128)(2,1)S(1)} %bundle.1.refs_1_, bf16[48,768]{1,0:T(8,128)(2,1)S(1)} %collective-permute-done.refs_2_, ...), custom_call_target="tpu_custom_call" | custom-call | tf_op jit(solution)/shard_map/pack/pallas_call | solution.py:357
  13.9 1.6 %collective-permute-start.6 = (bf16[4,3200]{1,0:T(4,128)(2,1)S(1)}, bf16[4,3200]{1,0:T(4,128)(2,1)S(1)}, u32[]{:S(2)}, u32[]{:S(2)}) collective-permute-start(bf16[4,3200]{1,0:T(4,128)(2,1)S(1)} %get-tuple-element.19.refs_0_), channel_id=1, source_target_pairs={{0,16},{4,20},{8,24},{12,28},{16,0},{20,4},{24,8},{28,12},{1,17},{... | collective-permute-start | bytes 76808 | tf_op jit(solution)/shard_map/ppermute | solution.py:374
  15.5 0.6 %collective-permute-start.3 = (bf16[4,3200]{1,0:T(4,128)(2,1)S(1)}, bf16[4,3200]{1,0:T(4,128)(2,1)S(1)}, u32[]{:S(2)}, u32[]{:S(2)}) collective-permute-start(bf16[4,3200]{1,0:T(4,128)(2,1)S(1)} %get-tuple-element.20), channel_id=1, source_target_pairs={{0,4},{4,0},{8,12},{12,8},{16,20},{20,16},{24,28},{28,24},{1,5},{5... | collective-permute-start | bytes 76808 | tf_op jit(solution)/shard_map/ppermute | solution.py:374
  16.1 2.4 %collective-permute-start.8 = (bf16[4,3200]{1,0:T(4,128)(2,1)S(1)}, bf16[4,3200]{1,0:T(4,128)(2,1)S(1)}, u32[]{:S(2)}, u32[]{:S(2)}) collective-permute-start(bf16[4,3200]{1,0:T(4,128)(2,1)S(1)} %get-tuple-element.21), channel_id=1, source_target_pairs={{0,24},{4,28},{8,16},{12,20},{16,8},{20,12},{24,0},{28,4},{1,25},{... | collective-permute-start | bytes 76808 | tf_op jit(solution)/shard_map/ppermute | solution.py:374
  18.5 0.5 collective-permute-start.4
  19.1 0.5 collective-permute-start.9
  19.5 1.2 %collective-permute-start.5 = (bf16[4,3200]{1,0:T(4,128)(2,1)S(1)}, bf16[4,3200]{1,0:T(4,128)(2,1)S(1)}, u32[]{:S(2)}, u32[]{:S(2)}) collective-permute-start(bf16[4,3200]{1,0:T(4,128)(2,1)S(1)} %get-tuple-element.22), channel_id=1, source_target_pairs={{0,12},{4,8},{8,4},{12,0},{16,28},{20,24},{24,20},{28,16},{1,13},{... | collective-permute-start | bytes 76808 | tf_op jit(solution)/shard_map/ppermute | solution.py:374
  20.8 0.1 collective-permute-done.8.refs_6_
  20.8 1.7 %collective-permute-done.4.refs_2_ = bf16[4,3200]{1,0:T(4,128)(2,1)S(1)} collective-permute-done((bf16[4,3200]{1,0:T(4,128)(2,1)S(1)}, bf16[4,3200]{1,0:T(4,128)(2,1)S(1)}, u32[]{:S(2)}, u32[]{:S(2)}) %collective-permute-start.4) | collective-permute-done | bytes 25632 | tf_op jit(solution)/shard_map/ppermute | solution.py:374
  22.6 0.7 %collective-permute-done.9.refs_7_ = bf16[4,3200]{1,0:T(4,128)(2,1)S(1)} collective-permute-done((bf16[4,3200]{1,0:T(4,128)(2,1)S(1)}, bf16[4,3200]{1,0:T(4,128)(2,1)S(1)}, u32[]{:S(2)}, u32[]{:S(2)}) %collective-permute-start.9) | collective-permute-done | bytes 25632 | tf_op jit(solution)/shard_map/ppermute | solution.py:374
  23.2 18.2 %main.1 = (bf16[32,2,1664]{2,1,0:T(2,128)(2,1)}, bf16[16,2048]{1,0:T(8,128)(2,1)S(1)}, bf16[16,2048]{1,0:T(8,128)(2,1)S(1)}, bf16[8,3072]{1,0:T(8,128)(2,1)S(1)}, bf16[8,32]{1,0:T(8,128)(2,1)S(1)}) custom-call(bf16[4,3200]{1,0:T(4,128)(2,1)S(1)} %get-tuple-element.19.refs_0_, bf16[4,3200]{1,0:T(4,128)(2,1)S(1)} %collective-permute-done.3.refs_1_, ...), custom_call_target="tpu_custom_call" | custom-call | flops 1006632960 | bytes 12582912 | tf_op jit(solution)/shard_map/main/pallas_call | solution.py:383
  41.4 4.4 %all-to-all-start = ((bf16[32,2,1664]{2,1,0:T(2,128)(2,1)}), bf16[32,2,1664]{2,1,0:T(2,128)(2,1)S(1)}, u32[]{:S(2)}, u32[]{:S(2)}) async-start(bf16[32,2,1664]{2,1,0:T(2,128)(2,1)} %get-tuple-element.26), calls=%async_computation | async-start | bytes 425984 | tf_op jit(solution)/shard_map/all_to_all | solution.py:422
  45.8 1.8 %collective-permute-start.10 = (bf16[16,2048]{1,0:T(8,128)(2,1)S(1)}, bf16[16,2048]{1,0:T(8,128)(2,1)S(1)}, u32[]{:S(2)}, u32[]{:S(2)}) collective-permute-start(bf16[16,2048]{1,0:T(8,128)(2,1)S(1)} %get-tuple-element.31), channel_id=1, source_target_pairs={{0,16},{16,0},{1,17},{17,1},{2,18},{18,2},{3,19},{19,3},{4,20},{20... | collective-permute-start | bytes 196616 | tf_op jit(solution)/shard_map/ppermute | solution.py:423
  47.7 3.6 %collective-permute-done.10.received = bf16[16,2048]{1,0:T(8,128)(2,1)S(1)} collective-permute-done((bf16[16,2048]{1,0:T(8,128)(2,1)S(1)}, bf16[16,2048]{1,0:T(8,128)(2,1)S(1)}, u32[]{:S(2)}, u32[]{:S(2)}) %collective-permute-start.10) | collective-permute-done | bytes 65568 | tf_op jit(solution)/shard_map/ppermute | solution.py:423
  51.3 1.1 %grad_up.1 = f32[2,16,4096]{2,1,0:T(8,128)} custom-call(bf16[16,2048]{1,0:T(8,128)(2,1)S(1)} %get-tuple-element.30.kept, bf16[16,2048]{1,0:T(8,128)(2,1)S(1)} %collective-permute-done.10.received, bf16[8,32]{1,0:T(8,128)(2,1)S(1)} %get-tuple-element.32.latent), custom_call_target="tpu_custom_call" | custom-call | flops 4194304 | bytes 524288 | tf_op jit(solution)/shard_map/grad_up/pallas_call | solution.py:424
  52.4 3.0 %all-to-all-done.received = bf16[32,2,1664]{2,1,0:T(2,128)(2,1)S(1)} async-done(((bf16[32,2,1664]{2,1,0:T(2,128)(2,1)}), bf16[32,2,1664]{2,1,0:T(2,128)(2,1)S(1)}, u32[]{:S(2)}, u32[]{:S(2)}) %all-to-all-start) | async-done | bytes 213024 | tf_op jit(solution)/shard_map/all_to_all | solution.py:422
  55.4 1.0 %last.1 = (bf16[1,3072]{1,0:T(2,128)(2,1)}, f32[32,768]{1,0:T(8,128)}) custom-call(bf16[32,2,1664]{2,1,0:T(2,128)(2,1)S(1)} %all-to-all-done.received, bf16[8,3072]{1,0:T(8,128)(2,1)S(1)} %get-tuple-element.27.x_cols), custom_call_target="tpu_custom_call" | custom-call | tf_op jit(solution)/shard_map/last/pallas_call | solution.py:444
  (6 shorter events, 0.0 us)
Async XLA Ops:
  1.5 10.4 %collective-permute-start.2 = (bf16[48,768]{1,0:T(8,128)(2,1)S(1)}, bf16[48,768]{1,0:T(8,128)(2,1)S(1)}, u32[]{:S(2)}, u32[]{:S(2)}) collective-permute-start(bf16[48,768]{1,0:T(8,128)(2,1)S(1)} %bundle.1.refs_1_), channel_id=1, source_target_pairs={{0,3},{1,2},{2,1},{3,0},{4,7},{5,6},{6,5},{7,4},{8,11},{9,10},{10,... | collective-permute-start | bytes 221192 | tf_op jit(solution)/shard_map/ppermute | solution.py:340
  6.6 6.2 %collective-permute-start.1 = (bf16[48,768]{1,0:T(8,128)(2,1)S(1)}, bf16[48,768]{1,0:T(8,128)(2,1)S(1)}, u32[]{:S(2)}, u32[]{:S(2)}) collective-permute-start(bf16[48,768]{1,0:T(8,128)(2,1)S(1)} %bundle.1.refs_1_), channel_id=1, source_target_pairs={{0,2},{1,3},{2,0},{3,1},{4,6},{5,7},{6,4},{7,5},{8,10},{9,11},{10,... | collective-permute-start | bytes 221192 | tf_op jit(solution)/shard_map/ppermute | solution.py:340
  6.6 6.2 %collective-permute-start = (bf16[48,768]{1,0:T(8,128)(2,1)S(1)}, bf16[48,768]{1,0:T(8,128)(2,1)S(1)}, u32[]{:S(2)}, u32[]{:S(2)}) collective-permute-start(bf16[48,768]{1,0:T(8,128)(2,1)S(1)} %bundle.1.refs_1_), channel_id=1, source_target_pairs={{0,1},{1,0},{2,3},{3,2},{4,5},{5,4},{6,7},{7,6},{8,9},{9,8},{10,11... | collective-permute-start | bytes 221192 | tf_op jit(solution)/shard_map/ppermute | solution.py:340
  13.9 5.2 %collective-permute-start.6 = (bf16[4,3200]{1,0:T(4,128)(2,1)S(1)}, bf16[4,3200]{1,0:T(4,128)(2,1)S(1)}, u32[]{:S(2)}, u32[]{:S(2)}) collective-permute-start(bf16[4,3200]{1,0:T(4,128)(2,1)S(1)} %get-tuple-element.19.refs_0_), channel_id=1, source_target_pairs={{0,16},{4,20},{8,24},{12,28},{16,0},{20,4},{24,8},{28,12},{1,17},{... | collective-permute-start | bytes 76808 | tf_op jit(solution)/shard_map/ppermute | solution.py:374
  15.5 4.1 %collective-permute-start.7 = (bf16[4,3200]{1,0:T(4,128)(2,1)S(1)}, bf16[4,3200]{1,0:T(4,128)(2,1)S(1)}, u32[]{:S(2)}, u32[]{:S(2)}) collective-permute-start(bf16[4,3200]{1,0:T(4,128)(2,1)S(1)} %get-tuple-element.20), channel_id=1, source_target_pairs={{0,20},{4,16},{8,28},{12,24},{16,4},{20,0},{24,12},{28,8},{1,21},{... | collective-permute-start | bytes 76808 | tf_op jit(solution)/shard_map/ppermute | solution.py:374
  15.5 5.3 %collective-permute-start.3 = (bf16[4,3200]{1,0:T(4,128)(2,1)S(1)}, bf16[4,3200]{1,0:T(4,128)(2,1)S(1)}, u32[]{:S(2)}, u32[]{:S(2)}) collective-permute-start(bf16[4,3200]{1,0:T(4,128)(2,1)S(1)} %get-tuple-element.20), channel_id=1, source_target_pairs={{0,4},{4,0},{8,12},{12,8},{16,20},{20,16},{24,28},{28,24},{1,5},{5... | collective-permute-start | bytes 76808 | tf_op jit(solution)/shard_map/ppermute | solution.py:374
  16.1 4.8 %collective-permute-start.8 = (bf16[4,3200]{1,0:T(4,128)(2,1)S(1)}, bf16[4,3200]{1,0:T(4,128)(2,1)S(1)}, u32[]{:S(2)}, u32[]{:S(2)}) collective-permute-start(bf16[4,3200]{1,0:T(4,128)(2,1)S(1)} %get-tuple-element.21), channel_id=1, source_target_pairs={{0,24},{4,28},{8,16},{12,20},{16,8},{20,12},{24,0},{28,4},{1,25},{... | collective-permute-start | bytes 76808 | tf_op jit(solution)/shard_map/ppermute | solution.py:374
  18.5 4.0 %collective-permute-start.4 = (bf16[4,3200]{1,0:T(4,128)(2,1)S(1)}, bf16[4,3200]{1,0:T(4,128)(2,1)S(1)}, u32[]{:S(2)}, u32[]{:S(2)}) collective-permute-start(bf16[4,3200]{1,0:T(4,128)(2,1)S(1)} %get-tuple-element.21), channel_id=1, source_target_pairs={{0,8},{4,12},{8,0},{12,4},{16,24},{20,28},{24,16},{28,20},{1,9},{5... | collective-permute-start | bytes 76808 | tf_op jit(solution)/shard_map/ppermute | solution.py:374
  19.1 4.2 %collective-permute-start.9 = (bf16[4,3200]{1,0:T(4,128)(2,1)S(1)}, bf16[4,3200]{1,0:T(4,128)(2,1)S(1)}, u32[]{:S(2)}, u32[]{:S(2)}) collective-permute-start(bf16[4,3200]{1,0:T(4,128)(2,1)S(1)} %get-tuple-element.22), channel_id=1, source_target_pairs={{0,28},{4,24},{8,20},{12,16},{16,12},{20,8},{24,4},{28,0},{1,29},{... | collective-permute-start | bytes 76808 | tf_op jit(solution)/shard_map/ppermute | solution.py:374
  19.5 3.7 %collective-permute-start.5 = (bf16[4,3200]{1,0:T(4,128)(2,1)S(1)}, bf16[4,3200]{1,0:T(4,128)(2,1)S(1)}, u32[]{:S(2)}, u32[]{:S(2)}) collective-permute-start(bf16[4,3200]{1,0:T(4,128)(2,1)S(1)} %get-tuple-element.22), channel_id=1, source_target_pairs={{0,12},{4,8},{8,4},{12,0},{16,28},{20,24},{24,20},{28,16},{1,13},{... | collective-permute-start | bytes 76808 | tf_op jit(solution)/shard_map/ppermute | solution.py:374
  41.4 14.0 %all-to-all-start = ((bf16[32,2,1664]{2,1,0:T(2,128)(2,1)}), bf16[32,2,1664]{2,1,0:T(2,128)(2,1)S(1)}, u32[]{:S(2)}, u32[]{:S(2)}) async-start(bf16[32,2,1664]{2,1,0:T(2,128)(2,1)} %get-tuple-element.26), calls=%async_computation | async-start | bytes 425984 | tf_op jit(solution)/shard_map/all_to_all | solution.py:422
  45.8 5.4 %collective-permute-start.10 = (bf16[16,2048]{1,0:T(8,128)(2,1)S(1)}, bf16[16,2048]{1,0:T(8,128)(2,1)S(1)}, u32[]{:S(2)}, u32[]{:S(2)}) collective-permute-start(bf16[16,2048]{1,0:T(8,128)(2,1)S(1)} %get-tuple-element.31), channel_id=1, source_target_pairs={{0,16},{16,0},{1,17},{17,1},{2,18},{18,2},{3,19},{19,3},{4,20},{20... | collective-permute-start | bytes 196616 | tf_op jit(solution)/shard_map/ppermute | solution.py:423
